TPU v7x, 256 devices: a whole 4x4x8 slice. The times are simulated.
256 devices in a mesh: dp: 64 (over y, z, core), mp: 4 (over x).
Axes of the slice: x: 4, y: 4, z: 8, core: 2. Of those that a mesh axis runs over, the one named last changes fastest.
Arguments:
- projected: bfloat16 [3, 8192, 3072], P(None, 'dp', 'mp'), may hold values from -32 to 32
- lengths: int32 [256], P('dp'), may hold values from 16 to 64, as said below
- owners: int32 [256], P('dp'), may hold values from 0 to 63, as said below
- cotangent: bfloat16 [16384, 6144], P('dp', 'mp'), may hold values from -0.125 to 0.125
Outputs:
- attended: bfloat16 [16384, 3072], P('dp', 'mp')
- out_grad: float32 [24, 128, 6144], P('mp', 'dp')
Inputs may be any that keep to these rules, and one draw needn't show every extreme that they name: `lengths`: each group's 4 images fill its 128 rows exactly; every group has one image of exactly 64 patches. `owners`: an image's owner is its own group or one of the two beside it (group 0 and the last group are neighbours); a group sends at most one image to each side; in some group the image sent right has 64 patches, and in some group the image sent left has.
All inputs are finite; a program needn't handle non-finite values.
Results may differ from a plain program's by a relative error of at most 0.0062.
Values may be sent and summed in bfloat16 or wider, within the bound.
A program may use at most 128 MiB of HBM per device.

v0:
```python
import jax
import jax.numpy as jnp
from jax import lax
from jax.sharding import PartitionSpec as P

HD = 128


def with_halo(block, sides, width):
    for axis, dim in sides:
        count = lax.axis_size(axis)
        forward = [(i, i + 1) for i in range(count - 1)]
        forward.append((count - 1, 0))
        backward = [(target, source) for source, target in forward]
        low = lax.ppermute(
            lax.slice_in_dim(block, block.shape[dim] - width, None, axis=dim), axis, forward
        )
        high = lax.ppermute(lax.slice_in_dim(block, 0, width, axis=dim), axis, backward)
        block = jnp.concatenate([low, block, high], axis=dim)
    return block


def passed_along(block, axis, distance):
    devices = range(lax.axis_size(axis))
    route = [((i - distance) % len(devices), i) for i in devices]
    return lax.ppermute(block, axis, route)


def norm_heads(values):
    centred = values - jnp.mean(values, axis=-1, keepdims=True)
    spread = jnp.mean(centred * centred, axis=-1, keepdims=True)
    return (centred * lax.rsqrt(spread + 1e-06)).astype(jnp.bfloat16)


def describe(image_info, count, group, groups):
    sizes = image_info[:count]
    heading = (image_info[count:] - group) % groups
    starts = jnp.cumsum(sizes) - sizes
    return (sizes, starts, heading)


def window_corner(sizes, starts, heading, target, span, rows):
    chosen = heading == target
    amount = jnp.sum(jnp.where(chosen, sizes, 0))
    first_row = jnp.sum(jnp.where(chosen, starts, 0))
    corner = jnp.minimum(first_row, rows - span)
    places = jnp.arange(span, dtype=jnp.int32)
    inside = (places >= first_row - corner) & (places < first_row - corner + amount)
    return (corner, inside)


def own_segments(sizes, starts, heading, rows):
    places = jnp.arange(rows, dtype=jnp.int32)
    image_of = jnp.sum((places[:, None] >= (starts + sizes)[None, :]).astype(jnp.int32), axis=1)
    matches = image_of[:, None] == jnp.arange(sizes.shape[0], dtype=jnp.int32)[None, :]
    staying = jnp.sum(jnp.where(matches, heading[None, :], 0), axis=1) == 0
    return jnp.where(staying, image_of, -1)


def attend_block(query_block, segment_block, keys_norm, values_all, segment_all):
    scores = jnp.einsum(
        "qhd,khd->hqk", query_block, keys_norm, preferred_element_type=jnp.float32
    ) * query_block.shape[-1] ** (-0.5)
    allowed = (segment_block[:, None] == segment_all[None, :]) & (segment_block[:, None] >= 0)
    raised = jnp.where(allowed[None], jnp.exp(scores), 0.0)
    totals = jnp.sum(raised, axis=-1, keepdims=True)
    weights = (raised / jnp.where((segment_block >= 0)[None, :, None], totals, 1.0)).astype(
        jnp.bfloat16
    )
    return jnp.einsum(
        "hqk,khd->qhd", weights, values_all, preferred_element_type=jnp.float32
    ).astype(jnp.bfloat16)


def shards(projected, lengths, owners, cotangent):
    groups = lax.axis_size("dp")
    position = lax.axis_index("dp")
    rows = projected.shape[1]
    span = rows // 2
    width = projected.shape[2]
    heads = width // HD
    count = lengths.shape[0]
    image_info = jnp.concatenate([lengths, owners])[None, :]
    beside = with_halo(image_info, (("dp", 0),), 1)
    mine = describe(beside[1], count, position, groups)
    before = describe(beside[0], count, (position - 1) % groups, groups)
    after = describe(beside[2], count, (position + 1) % groups, groups)
    right_corner, unused_right = window_corner(mine[0], mine[1], mine[2], 1, span, rows)
    left_corner, unused_left = window_corner(mine[0], mine[1], mine[2], groups - 1, span, rows)
    unused_before, inside_left = window_corner(before[0], before[1], before[2], 1, span, rows)
    unused_after, inside_right = window_corner(after[0], after[1], after[2], groups - 1, span, rows)
    going_right = lax.dynamic_slice_in_dim(projected, right_corner, span, 1)
    going_left = lax.dynamic_slice_in_dim(projected, left_corner, span, 1)
    arrived = []
    for offset, outgoing in ((1, going_right), (-1, going_left)):
        arrived.append(passed_along(outgoing, "dp", offset))
    from_left = arrived[0]
    from_right = arrived[1]
    packed = jnp.concatenate([projected, from_left, from_right], axis=1)
    segment = jnp.concatenate(
        [
            own_segments(mine[0], mine[1], mine[2], rows),
            jnp.where(inside_left, 4, -1).astype(jnp.int32),
            jnp.where(inside_right, 5, -1).astype(jnp.int32),
        ]
    )
    packed_rows = packed.shape[1]
    queries = norm_heads(packed[0].astype(jnp.float32).reshape(packed_rows, heads, HD))
    keys_norm = norm_heads(packed[1].astype(jnp.float32).reshape(packed_rows, heads, HD))
    values_all = packed[2].reshape(packed_rows, heads, HD)
    block_rows = min(512, packed_rows)
    block_count = packed_rows // block_rows

    def one_block(inputs_pair):
        return attend_block(inputs_pair[0], inputs_pair[1], keys_norm, values_all, segment)

    attended = lax.map(
        one_block,
        (
            queries.reshape(block_count, block_rows, heads, HD),
            segment.reshape(block_count, block_rows),
        ),
    )
    attended = attended.reshape(packed_rows, width)
    share_rows = HD // groups
    head_sets = 3
    head_step = heads // head_sets
    columns = lax.all_gather(cotangent, "mp", axis=1, tiled=True)
    head_cube = attended.reshape(packed_rows, heads, HD)
    pieces = []
    for index in range(head_sets):
        cube_part = head_cube[:, index * head_step : (index + 1) * head_step, :]

        def grad_term(start, amount, cube_part=cube_part):
            return jnp.einsum("phc,pe->che", cube_part, columns, preferred_element_type=jnp.float32)

        pieces.append(
            lax.psum_scatter(
                grad_term(jnp.int32(0), share_rows * lax.axis_size("dp")),
                "dp",
                scatter_dimension=0,
                tiled=True,
            )
        )
    summed = jnp.concatenate(pieces, axis=1)
    result_grad = jnp.transpose(summed, (1, 0, 2))
    return (attended, result_grad)


def solution(mesh):
    return jax.shard_map(
        shards,
        mesh=mesh,
        in_specs=(P(None, "dp", "mp"), P("dp"), P("dp"), P("dp", "mp")),
        out_specs=(P("dp", "mp"), P("mp", "dp", None)),
        check_vma=False,
    )
```

profile of v0, /device:TPU:1, one launch (start us, length us, event | category | flops | bytes accessed | tf_op | source)
XLA Modules:
  0.0 318.9 jit_solution(2566703436200662187)
XLA Ops:
  7.2 0.7 all-gather.2.cloned.1.call-update
  7.9 0.7 add_bitcast_fusion
  8.7 3.0 collective-permute-start.2
  11.7 0.3 collective-permute-start.3
  12.0 0.8 reduce-window.26
  12.8 1.3 fusion.24
  15.5 1.2 constant_dynamic-slice_fusion.4
  16.7 1.5 collective-permute-start
  18.2 4.7 %collective-permute-start.1 = (bf16[3,64,768]{2,1,0:T(8,128)(2,1)S(1)}, bf16[3,64,768]{2,1,0:T(8,128)(2,1)S(1)}, u32[]{:S(2)}, u32[]{:S(2)}) collective-permute-start(bf16[3,64,768]{2,1,0:T(8,128)(2,1)S(1)} %get-tuple-element.47), channel_id=1, source_target_pairs={{4,0},{8,4},{12,8},{16,12},{20,16},{24,20},{28,24},{32,28},{36,32}... | collective-permute-start | bytes 884744 | tf_op jit(solution)/shard_map/ppermute | solution.py:26
  22.9 1.4 copy.25
  24.5 0.2 reduce-window.27
  24.7 0.8 fusion.21
  26.8 0.2 reduce-window.28
  27.0 0.7 fusion.23
  30.6 0.3 copy.26
  30.9 0.3 copy.27
  31.3 0.4 pad_maximum_fusion
  32.0 0.1 fusion.7
  32.2 0.6 fusion.30
  32.8 0.3 convolution_convert_fusion
  33.0 22.6 %all-gather.2.cloned.1.call-done = bf16[256,6144]{1,0:T(8,128)(2,1)} async-done(((bf16[256,1536]{1,0:T(8,128)(2,1)}), bf16[256,6144]{1,0:T(8,128)(2,1)}) %all-gather.2.cloned.1.call-update) | async-done | bytes 3145744 | tf_op jit(solution)/shard_map/all_gather | solution.py:128
  55.7 5.7 %convolution_bitcast_fusion = f32[128,2,6144]{2,0,1:T(8,128)} fusion(bf16[256,6144]{1,0:T(8,128)(2,1)} %all-gather.2.cloned.1.call-done, bf16[6,128,256]{2,1,0:T(8,128)(2,1)S(1)} %convolution_convert_fusion), kind=kOutput, calls=%fused_computation | convolution fusion | flops 805306368 | bytes 9830400 | tf_op jit(solution)/shard_map/phc,pe->che/dot_general | solution.py:135
  61.4 3.7 %convolution_bitcast_fusion.1 = f32[128,2,6144]{2,0,1:T(8,128)} fusion(bf16[256,6144]{1,0:T(8,128)(2,1)S(1)} %copy-done, bf16[6,128,256]{2,1,0:T(8,128)(2,1)S(1)} %convolution_convert_fusion), kind=kOutput, calls=%fused_computation.1 | convolution fusion | flops 805306368 | bytes 9830400 | tf_op jit(solution)/shard_map/phc,pe->che/dot_general | solution.py:135
  65.1 3.7 %convolution_bitcast_fusion.2 = f32[128,2,6144]{2,0,1:T(8,128)} fusion(bf16[256,6144]{1,0:T(8,128)(2,1)S(1)} %copy-done, bf16[6,128,256]{2,1,0:T(8,128)(2,1)S(1)} %convolution_convert_fusion), kind=kOutput, calls=%fused_computation.2 | convolution fusion | flops 805306368 | bytes 9830400 | tf_op jit(solution)/shard_map/phc,pe->che/dot_general | solution.py:135
  68.8 0.6 copy-done.1
  69.5 0.6 dynamic-slice.2
  70.7 0.9 copy.31
  71.6 236.5 %all-reduce.6.cloned.1.call-done = (f32[128,2,6144]{2,0,1:T(8,128)}, f32[128,2,6144]{2,0,1:T(8,128)}, f32[128,2,6144]{2,0,1:T(8,128)}) async-done(((f32[128,2,6144]{2,0,1:T(8,128)}, f32[128,2,6144]{2,0,1:T(8,128)}, f32[128,2,6144]{2,0,1:T(8,128)}), (f32[128,2,6144]{2,0,1:T(8,128)}, f32[128,2,6144]{2,0,1:T(8,128)}, f32[128,2,6144]{2,0,1:T(8,128)})) %all-reduce.6.cloned.1.call-update) | async-done | bytes 18874384
  308.1 1.0 constant_dynamic-slice_fusion
  309.2 1.0 constant_dynamic-slice_fusion.1
  310.2 1.0 constant_dynamic-slice_fusion.2
  311.2 0.8 maximum_bitcast_fusion
  (26 shorter events, 0.8 us)
Async XLA Ops:
  7.2 48.5 %all-gather.2.cloned.1.call-start = ((), (), s32[]{:S(2)}) async-start(), calls=%async_computation | async-start | bytes 3932160 | tf_op jit(solution)/shard_map/all_gather | solution.py:128
  7.9 300.2 %all-reduce.6.cloned.1.call-start = ((), (), s32[]{:S(2)}) async-start(), calls=%async_computation.1 | async-start | bytes 37748736
  8.7 15.8 %collective-permute-start.2 = (s32[1,8]{1,0:T(1,128)S(1)}, s32[1,8]{1,0:T(1,128)S(1)}, u32[]{:S(2)}, u32[]{:S(2)}) collective-permute-start(s32[1,8]{1,0:T(1,128)S(1)} %add_bitcast_fusion), channel_id=1, source_target_pairs={{0,4},{4,8},{8,12},{12,16},{16,20},{20,24},{24,28},{28,32},{32,36}... | collective-permute-start | bytes 104 | tf_op jit(solution)/shard_map/ppermute | solution.py:15
  11.7 15.1 %collective-permute-start.3 = (s32[1,8]{1,0:T(1,128)S(1)}, s32[1,8]{1,0:T(1,128)S(1)}, u32[]{:S(2)}, u32[]{:S(2)}) collective-permute-start(s32[1,8]{1,0:T(1,128)S(1)} %add_bitcast_fusion), channel_id=1, source_target_pairs={{4,0},{8,4},{12,8},{16,12},{20,16},{24,20},{28,24},{32,28},{36,32}... | collective-permute-start | bytes 104 | tf_op jit(solution)/shard_map/ppermute | solution.py:18
  16.7 13.8 %collective-permute-start = (bf16[3,64,768]{2,1,0:T(8,128)(2,1)S(1)}, bf16[3,64,768]{2,1,0:T(8,128)(2,1)S(1)}, u32[]{:S(2)}, u32[]{:S(2)}) collective-permute-start(bf16[3,64,768]{2,1,0:T(8,128)(2,1)S(1)} %get-tuple-element.46), channel_id=1, source_target_pairs={{252,0},{0,4},{4,8},{8,12},{12,16},{16,20},{20,24},{24,28},{28,32}... | collective-permute-start | bytes 884744 | tf_op jit(solution)/shard_map/ppermute | solution.py:26
  18.2 12.7 %collective-permute-start.1 = (bf16[3,64,768]{2,1,0:T(8,128)(2,1)S(1)}, bf16[3,64,768]{2,1,0:T(8,128)(2,1)S(1)}, u32[]{:S(2)}, u32[]{:S(2)}) collective-permute-start(bf16[3,64,768]{2,1,0:T(8,128)(2,1)S(1)} %get-tuple-element.47), channel_id=1, source_target_pairs={{4,0},{8,4},{12,8},{16,12},{20,16},{24,20},{28,24},{32,28},{36,32}... | collective-permute-start | bytes 884744 | tf_op jit(solution)/shard_map/ppermute | solution.py:26
  55.7 5.7 %copy-start = (bf16[256,6144]{1,0:T(8,128)(2,1)S(1)}, bf16[256,6144]{1,0:T(8,128)(2,1)}, u32[]{:S(2)}) copy-start(bf16[256,6144]{1,0:T(8,128)(2,1)} %all-gather.2.cloned.1.call-done) | copy-start | bytes 9437188
  68.8 0.7 copy-start.1
Sparse Core Ops, SparseCore 0:
  9.8 45.8 all-gather.1
  69.0 239.1 all-reduce.5
where the time goes:
time: 319 us
  waiting for transfers between devices  260 us (82%)
  between operations  20.2 us (6%)
  matrix products  14 us (4%)
  starting transfers between devices  9.58 us (3%)
  local copies, waits for them, and re-layouts  8.64 us (3%)
  other arithmetic  6.74 us (2%)
    unnamed x3, waiting for transfers between devices  237 us
    all_gather x1, waiting for transfers between devices, shards(): columns = lax.all_gather(cotangent, 'mp', axis=1, tiled=True)  22.6 us
    dot_general x3, matrix products, grad_term(): jnp.einsum('phc,pe->che', cube_part, columns, preferred_element_type=jnp....  13.1 us
    unnamed x10, local copies, waits for them, and re-layouts  6.66 us
  transfers between devices with their start and end apart: 6, of which 2 were waited for; matrix products, arithmetic and copies ran while one was open for 4% of the time, Pallas kernels for 0%

commit v1 on v0

v1 whole, which is shorter than its diff:
```python
import functools

import jax
import jax.numpy as jnp
from jax import lax
from jax.experimental import pallas as pl
from jax.experimental.pallas import tpu as pltpu
from jax.sharding import PartitionSpec as P

MESH = pl.DeviceIdType.MESH
BF16 = jnp.bfloat16
F32 = jnp.float32
NX, NY, NZ = 4, 4, 8
HD = 128
HEADS = 6
WIDTH = HEADS * HD
ROWS = 128
SPAN = 64
PACK = 256
IMGS = 4
GROUPS = 2 * NY * NZ
FEAT = 1536
HALF = FEAT // 2
CHUNK = 256
SHARE = 24
D = 6144
RING = {"y": NY, "z": NZ}
BLOCK = {"y": NZ * SHARE, "z": NY * SHARE}

UNITS = [
    (0, 0, "y"), (0, 1, "z"), (1, 0, "y"), (3, 0, "z"), (1, 1, "y"), (3, 1, "y"),
    (1, 2, "z"), (3, 2, "y"), (2, 0, "y"), (2, 1, "z"), (2, 2, "y"), (0, 2, "z"),
]


def place():
    dp = lax.axis_index("dp")
    chip = dp // 2
    return chip // NZ, chip % NZ, dp % 2, lax.axis_index("mp")


def device(y, z, core, x):
    return ((y % NY * NZ + z % NZ) * 2 + core, x % NX)


def plan_steps():
    ready = {("A", 0): 8.0, ("A", 1): 15.5, ("A", 3): 15.5, ("A", 2): 19.5}
    tasks = {}
    for u, (r, fu, first) in enumerate(UNITS):
        second = "z" if first == "y" else "y"
        h1, h2 = RING[first] // 2, RING[second] // 2
        size = BLOCK[first] * CHUNK * 2
        tasks[("M", u)] = ([("A", r)], 0.5, None)
        for k in range(h1):
            for s in (0, 1):
                needs = [("M", u)] + ([("R1", u, s, k - 1)] if k else [])
                sent = size // 2 if k == 0 else size
                tasks[("S1", u, s, k)] = (needs, 0.1, (("R1", u, s, k), first, s, sent))
        tasks[("F1", u)] = ([("R1", u, 0, h1 - 1), ("R1", u, 1, h1 - 1)], 0.1, None)
        for k in range(h2):
            for s in (0, 1):
                if k == 0 and s != u % 2:
                    continue
                needs = [("F1", u)]
                if k > 1 or (k == 1 and s == u % 2):
                    needs.append(("R2", u, s, k - 1))
                tasks[("S2", u, s, k)] = (needs, 0.1, (("R2", u, s, k), second, s, 12288))
        tasks[("F2", u)] = ([("R2", u, 0, h2 - 1), ("R2", u, 1, h2 - 1)], 0.1, None)
    depth = {"M": 0, "S1": 1, "F1": 6, "S2": 7, "F2": 12}

    def rank(name):
        return (name[1], -depth[name[0]] - (name[3] if len(name) > 2 else 0), name[2:])

    done = dict(ready)
    links = {}
    now = 8.0
    order = []
    while tasks:
        best = None
        for name, (needs, _, _) in tasks.items():
            if all(n in done for n in needs):
                at = max(done[n] for n in needs)
                key = (0, 0.0) if at <= now else (1, at)
                if best is None or (key, rank(name)) < best[0]:
                    best = ((key, rank(name)), name, at)
        _, name, at = best
        _, spent, message = tasks.pop(name)
        now = max(now, at) + spent
        done[name] = now
        order.append(name)
        if message:
            label, axis, s, size = message
            end = max(links.get((axis, s), 0.0), now) + size / 50e3
            links[(axis, s)] = end
            done[label] = end + 1.7
    return order


def attend(len_ref, own_ref, proj_ref, group, att):
    lens = [len_ref[j] for j in range(IMGS)]
    ends = [lens[0], lens[0] + lens[1], lens[0] + lens[1] + lens[2]]
    starts = [jnp.int32(0)] + ends
    stops = ends + [ends[2] + lens[3]]
    row = lax.broadcasted_iota(jnp.int32, (ROWS, ROWS), 0)
    col = lax.broadcasted_iota(jnp.int32, (ROWS, ROWS), 1)

    def image(at):
        return sum((at >= e).astype(jnp.int32) for e in ends)

    same = image(row) == image(col)
    scale = HD ** (-0.5)

    def norm(values):
        values = values.astype(F32)
        centred = values - jnp.mean(values, axis=-1, keepdims=True)
        spread = jnp.mean(centred * centred, axis=-1, keepdims=True)
        return (centred * lax.rsqrt(spread + 1e-06)).astype(BF16)

    for h in range(HEADS):
        lanes = slice(h * HD, (h + 1) * HD)
        q = norm(proj_ref[0, :, lanes])
        k = norm(proj_ref[1, :, lanes])
        scores = lax.dot_general(q, k, (((1,), (1,)), ((), ())), preferred_element_type=F32) * scale
        raised = jnp.where(same, jnp.exp(scores), 0.0)
        totals = jnp.sum(raised, axis=-1, keepdims=True)
        weights = (raised / totals).astype(BF16)
        out = jnp.dot(weights, proj_ref[2, :, lanes], preferred_element_type=F32)
        att[:, lanes] = out.astype(BF16)

    stays = jnp.zeros((ROWS, ROWS), jnp.bool_)
    for j in range(IMGS):
        stays = stays | ((row >= starts[j]) & (row < stops[j]) & (own_ref[j] == group))
    picks = [jnp.where((row == col) & stays, 1.0, 0.0).astype(BF16)]
    row64 = lax.broadcasted_iota(jnp.int32, (SPAN, ROWS), 0)
    col64 = lax.broadcasted_iota(jnp.int32, (SPAN, ROWS), 1)
    for step in (1, GROUPS - 1):
        target = (group + step) % GROUPS
        first = jnp.int32(0)
        stop = jnp.int32(0)
        for j in range(IMGS):
            chosen = own_ref[j] == target
            first = first + jnp.where(chosen, starts[j], 0)
            stop = stop + jnp.where(chosen, stops[j], 0)
        corner = jnp.minimum(first, ROWS - SPAN)
        pick = (col64 == row64 + corner) & (col64 >= first) & (col64 < stop)
        picks.append(jnp.where(pick, 1.0, 0.0).astype(BF16))
    return picks


def order_matrix(y, z):
    i = lax.broadcasted_iota(jnp.int32, (WIDTH, HD), 0)
    lane = lax.broadcasted_iota(jnp.int32, (WIDTH, HD), 1)
    block = (i * 2731) >> 16
    inner = i - SHARE * block
    core = (inner >= SHARE // 2).astype(jnp.int32)
    inner = inner - (SHARE // 2) * core
    yd = ((block >> 3) + y) & (NY - 1)
    zd = ((block & (NZ - 1)) + z) & (NZ - 1)
    d = ((yd * NZ + zd) * 2 + core) * 2 + (inner & 1)
    head = inner >> 1
    return [jnp.where((lane == d) & (head == h), 1.0, 0.0).astype(BF16) for h in range(HEADS)]


def kernel(
    steps, len_ref, own_ref, proj_ref, cot_ref, att_out, grad_out,
    att, outb, cotb, gathered, order, turned, partial, sum1_out, sum1_in, sum2, sum2_out, sum2_in, final, grads,
    send_sem, recv_sem, local_sem,
):
    y, z, core, x = place()
    other = 1 - core
    group = (y * NZ + z) * 2 + core
    chip = y * NZ + z
    after = (chip + 1) % (NY * NZ)
    before = (chip + NY * NZ - 1) % (NY * NZ)

    def at_chip(c, which):
        return (c * 2 + which, x)

    sibling = device(y, z, other, x)
    near = {
        ("y", 0): device(y + 1, z, core, x), ("y", 1): device(y + NY - 1, z, core, x),
        ("z", 0): device(y, z + 1, core, x), ("z", 1): device(y, z + NZ - 1, core, x),
        ("x", 0): device(y, z, core, x + 1), ("x", 1): device(y, z, core, x + NX - 1),
    }
    partners = [sibling] + list(near.values())
    partners += [at_chip(c, which) for c in (after, before) for which in (0, 1)]
    partners += [device(y, z, other, x + 1), device(y, z, other, x + NX - 1)]
    partners += [device(y, z, core, x + 2), device(y, z, other, x + 2)]
    barrier = pltpu.get_barrier_semaphore()
    for p in partners:
        pl.semaphore_signal(barrier, inc=1, device_id=p, device_id_type=MESH)

    counter = [0]
    sent = []

    def message(src, dst, target):
        n = counter[0]
        counter[0] += 1
        copy = pltpu.make_async_remote_copy(
            src_ref=src, dst_ref=dst, send_sem=send_sem.at[n], recv_sem=recv_sem.at[n],
            device_id=target, device_id_type=MESH,
        )
        copy.start()
        sent.append(copy)
        return copy

    def rows(start, size):
        return pl.ds(pl.multiple_of(start, 64), size)

    own_rows = rows(core * PACK, PACK)
    lanes = pl.ds(pl.multiple_of(core * HALF, HALF), HALF)
    lanes_other = pl.ds(pl.multiple_of(other * HALF, HALF), HALF)
    cot_here = pltpu.make_async_copy(cot_ref.at[:, lanes], cotb.at[own_rows], local_sem.at[0])
    cot_here.start()

    picks = attend(len_ref, own_ref, proj_ref, group, att)
    stay_rows = rows(core * PACK, ROWS)
    for n, pick in enumerate(picks):
        part = jnp.dot(pick, att[...], preferred_element_type=F32).astype(BF16)
        size = pick.shape[0]
        start = 0 if n == 0 else ROWS + SPAN * (n - 1)
        outb[start : start + size] = part
        if n == 0:
            gathered[0, stay_rows] = part

    pl.semaphore_wait(barrier, len(partners))

    inner_src = outb.at[rows(ROWS + SPAN * core, SPAN)]
    outer_src = outb.at[rows(ROWS + SPAN * other, SPAN)]
    inner_dst = rows((PACK + ROWS) * other + (ROWS + SPAN) * core, SPAN)
    outer_dst = rows((PACK + ROWS + SPAN) * other + ROWS * core, SPAN)
    outer_chip = before * other + after * core
    inner_here = pltpu.make_async_copy(inner_src, gathered.at[0, inner_dst], local_sem.at[1])
    inner_here.start()
    left_rows = pl.ds(ROWS, SPAN)
    right_rows = pl.ds(PACK + ROWS + SPAN, SPAN)
    outer = []
    base = counter[0]
    for which in (0, 1):
        copy = pltpu.make_async_remote_copy(
            src_ref=outer_src, dst_ref=gathered.at[0, outer_dst],
            send_sem=send_sem.at[base + which], recv_sem=recv_sem.at[base + core],
            device_id=at_chip(outer_chip, which), device_id_type=MESH,
        )
        copy.start()
        sent.append(copy)
    counter[0] += 2
    for which, place_in in ((0, right_rows), (1, left_rows)):
        outer.append(
            pltpu.make_async_remote_copy(
                src_ref=outb.at[pl.ds(0, SPAN)], dst_ref=gathered.at[0, place_in],
                send_sem=send_sem.at[base + which], recv_sem=recv_sem.at[base + which],
                device_id=sibling, device_id_type=MESH,
            )
        )
    first_half = rows(core * PACK, ROWS)
    second_half = rows(core * PACK + ROWS, ROWS)
    stay_cp = message(outb.at[pl.ds(0, ROWS)], gathered.at[0, stay_rows], sibling)
    inner_cp = message(inner_src, gathered.at[0, inner_dst], sibling)
    plus_a = message(gathered.at[0, first_half], gathered.at[3, first_half], near[("x", 0)])
    minus_a = message(gathered.at[0, first_half], gathered.at[1, first_half], near[("x", 1)])
    cot_cp = message(cot_ref.at[:, lanes_other], cotb.at[own_rows], sibling)

    for h, piece in enumerate(order_matrix(y, z)):
        order[:, h * HD : (h + 1) * HD] = piece

    inner_here.wait()
    inner_cp.wait_recv()
    for copy in outer:
        copy.wait_recv()
    plus_b = message(gathered.at[0, second_half], gathered.at[3, second_half], near[("x", 0)])
    minus_b = message(gathered.at[0, second_half], gathered.at[1, second_half], near[("x", 1)])
    stay_cp.wait_recv()

    def turn(r):
        for b in range(0, WIDTH, PACK):
            turned[r, b : b + PACK] = lax.dot_general(
                order[b : b + PACK], gathered[r], (((1,), (1,)), ((), ())), preferred_element_type=F32
            ).astype(BF16)

    turn(0)
    att_out[...] = gathered[0, own_rows]
    cot_here.wait()
    cot_cp.wait_recv()

    passed = {}

    def relay_near():
        plus_a.wait_recv()
        minus_a.wait_recv()
        relay_plus = message(gathered.at[3, first_half], gathered.at[2, first_half], near[("x", 0)])
        plus_b.wait_recv()
        minus_b.wait_recv()
        relay_minus = message(gathered.at[1, second_half], gathered.at[2, second_half], near[("x", 1)])
        passed[3] = message(gathered.at[3, own_rows], gathered.at[3, own_rows], sibling)
        passed[1] = message(gathered.at[1, own_rows], gathered.at[1, own_rows], sibling)
        passed["far"] = (relay_plus, relay_minus)

    def relay_far():
        for copy in passed["far"]:
            copy.wait_recv()
        passed[2] = message(gathered.at[2, own_rows], gathered.at[2, own_rows], sibling)

    ready = {0}
    received = {}
    slots = {}
    used = {"y": 0, "z": 0}
    for u, (r, fu, first) in enumerate(UNITS):
        slots[u] = used[first]
        used[first] += 1

    def region1(u, s, k):
        first = UNITS[u][2]
        size = BLOCK[first]
        if k == 0:
            return pl.ds(0, size // 2)
        return pl.ds(size // 2 + (k - 1) * size, size)

    def own1(u, rel):
        first = UNITS[u][2]
        if first == "y":
            return partial[u, rel * BLOCK["y"] : (rel + 1) * BLOCK["y"]]
        per = BLOCK["y"]
        return jnp.concatenate(
            [partial[u, b * per + rel * SHARE : b * per + (rel + 1) * SHARE] for b in range(NY)], axis=0
        )

    def do_multiply(u):
        r, fu, _ = UNITS[u]
        if r not in ready:
            if r == 2:
                passed[2].wait_recv()
            else:
                passed[r].wait_recv()
            turn(r)
            ready.add(r)
        partial[u] = jnp.dot(
            turned[r], cotb[:, fu * CHUNK : (fu + 1) * CHUNK], preferred_element_type=F32
        )

    def do_first(u, s, k):
        first = UNITS[u][2]
        n = RING[first]
        far = n // 2 - k
        rel = far if s == 0 else (n - far) % n
        mine = own1(u, rel)
        size = BLOCK[first]
        out = sum1_out[first].at[slots[u], s, region1(u, s, k)]
        if k == 0:
            half = size // 2
            out[...] = mine[s * half : (s + 1) * half].astype(BF16)
        else:
            received[(1, u, s, k - 1)].wait_recv()
            got = sum1_in[first][slots[u], s, region1(u, s, k - 1)].astype(F32)
            if k == 1:
                half = size // 2
                parts = [mine[:half], mine[half:]]
                parts[s] = parts[s] + got
                total = jnp.concatenate(parts, axis=0)
            else:
                total = mine + got
            out[...] = total.astype(BF16)
        received[(1, u, s, k)] = message(out, sum1_in[first].at[slots[u], s, region1(u, s, k)], near[(first, s)])

    def do_turn(u):
        first, n2 = UNITS[u][2], RING["z" if UNITS[u][2] == "y" else "y"]
        k = RING[first] // 2 - 1
        total = own1(u, 0)
        for s in (0, 1):
            received[(1, u, s, k)].wait_recv()
            total = total + sum1_in[first][slots[u], s, region1(u, s, k)].astype(F32)
        for b in range(n2):
            block = total[b * SHARE : (b + 1) * SHARE]
            sum2[u, b] = jnp.concatenate([block[:, :HD], block[:, HD:]], axis=0)

    def do_second(u, s, k):
        second = "z" if UNITS[u][2] == "y" else "y"
        n = RING[second]
        far = n // 2 - k
        rel = far if s == 0 else (n - far) % n
        total = sum2[u, rel]
        if (2, u, s, k - 1) in received:
            received[(2, u, s, k - 1)].wait_recv()
            total = total + sum2_in[u, s, k - 1].astype(F32)
        sum2_out[u, s, k] = total.astype(BF16)
        received[(2, u, s, k)] = message(sum2_out.at[u, s, k], sum2_in.at[u, s, k], near[(second, s)])

    arriving = []

    def do_last(u):
        r, fu, first = UNITS[u]
        k = RING["z" if first == "y" else "y"] // 2 - 1
        total = sum2[u, 0]
        for s in (0, 1):
            received[(2, u, s, k)].wait_recv()
            total = total + sum2_in[u, s, k].astype(F32)
        part = SHARE // 2
        for c in (0, 1):
            for side in (0, 1):
                start = side * SHARE + c * part
                final[u, c, 0:part, side * HD : (side + 1) * HD] = total[start : start + part]
        here = pl.ds(pl.multiple_of(x * FEAT + core * HALF + fu * CHUNK, CHUNK), CHUNK)
        if r == 0:
            copy = pltpu.make_async_copy(final.at[u, core], grads.at[:, here], local_sem.at[2 + fu])
            copy.start()
            arriving.append((copy, True))
        else:
            arriving.append((message(final.at[u, core], grads.at[:, here], device(y, z, core, x + r)), False))
        arriving.append((message(final.at[u, other], grads.at[:, here], device(y, z, other, x + r)), False))

    near_done = far_done = False
    for name in steps:
        kind, u = name[0], name[1]
        if not near_done and kind == "M" and UNITS[u][0] != 0:
            relay_near()
            near_done = True
        if not far_done and kind == "M" and UNITS[u][0] == 2:
            relay_far()
            far_done = True
        if kind == "M":
            do_multiply(u)
        elif kind == "S1":
            do_first(*name[1:])
        elif kind == "F1":
            do_turn(u)
        elif kind == "S2":
            do_second(*name[1:])
        else:
            do_last(u)

    for copy, local in arriving:
        if local:
            copy.wait()
        else:
            copy.wait_recv()
    grad_out[...] = grads[0 : SHARE // 2]
    for copy in sent:
        copy.wait_send()


def shards(projected, lengths, owners, cotangent):
    steps = plan_steps()
    units = len(UNITS)
    counts = {a: sum(1 for unit in UNITS if unit[2] == a) for a in ("y", "z")}
    lead = {a: BLOCK[a] // 2 + (RING[a] // 2 - 1) * BLOCK[a] for a in ("y", "z")}
    messages = 160
    sums = {a: pltpu.VMEM((counts[a], 2, lead[a], CHUNK), BF16) for a in ("y", "z")}
    vmem = pl.BlockSpec(memory_space=pltpu.VMEM)
    smem = pl.BlockSpec(memory_space=pltpu.SMEM)
    scratch = [
        pltpu.VMEM((ROWS, WIDTH), BF16),
        pltpu.VMEM((PACK, WIDTH), BF16),
        pltpu.VMEM((2 * PACK, HALF), BF16),
        pltpu.VMEM((NX, 2 * PACK, WIDTH), BF16),
        pltpu.VMEM((WIDTH, WIDTH), BF16),
        pltpu.VMEM((NX, WIDTH, 2 * PACK), BF16),
        pltpu.VMEM((units, WIDTH, CHUNK), F32),
        sums,
        sums,
        pltpu.VMEM((units, NZ, 2 * SHARE, HD), F32),
        pltpu.VMEM((units, 2, NZ // 2, 2 * SHARE, HD), BF16),
        pltpu.VMEM((units, 2, NZ // 2, 2 * SHARE, HD), BF16),
        pltpu.VMEM((units, 2, 16, CHUNK), F32),
        pltpu.VMEM((16, D), F32),
        pltpu.SemaphoreType.DMA((messages + 40,)),
        pltpu.SemaphoreType.DMA((messages + 40,)),
        pltpu.SemaphoreType.DMA((8,)),
    ]
    attended, grads = pl.pallas_call(
        functools.partial(kernel, steps),
        out_shape=(
            jax.ShapeDtypeStruct((PACK, WIDTH), BF16),
            jax.ShapeDtypeStruct((SHARE // 2, D), F32),
        ),
        in_specs=[smem, smem, vmem, pl.BlockSpec(memory_space=pl.ANY)],
        out_specs=(vmem, vmem),
        scratch_shapes=scratch,
        compiler_params=pltpu.CompilerParams(
            collective_id=0, has_side_effects=True, vmem_limit_bytes=56 * 2**20
        ),
        name="attend_and_reduce",
    )(lengths, owners, projected, cotangent)
    return attended, grads.reshape(HEADS, 2, D)


def solution(mesh):
    return jax.shard_map(
        shards,
        mesh=mesh,
        in_specs=(P(None, "dp", "mp"), P("dp"), P("dp"), P("dp", "mp")),
        out_specs=(P("dp", "mp"), P("mp", "dp", None)),
        check_vma=False,
    )
```

time: 319 us -> 80.2 us (0.25)
  waiting for transfers between devices: 260 us -> 0 us
  Pallas kernels: 0 us -> 76.7 us
  between operations: 20.2 us -> 0.65 us
  matrix products: 14 us -> 0 us
  starting transfers between devices: 9.58 us -> 0 us
  other arithmetic: 6.74 us -> 0 us
  local copies, waits for them, and re-layouts: 8.64 us -> 2.68 us
    unnamed x3 -> x0, waiting for transfers between devices: 237 us -> none
    pallas_call x0 -> x1, Pallas kernels: none -> 76.7 us  [shards(): pl.pallas_call(functools.partial(kernel, steps), out_shape=(jax.ShapeDtyp...]
    all_gather x1 -> x0, waiting for transfers between devices: 22.6 us -> none  [shards(): columns = lax.all_gather(cotangent, 'mp', axis=1, tiled=True)]
    dot_general x5 -> x0, matrix products: 14 us -> none  [the longest x3 13.1 us: grad_term(): jnp.einsum('phc,pe->che', cube_part, columns, preferred_element_type=jnp....]
    ppermute x4 -> x0, starting transfers between devices: 9.5 us -> none  [the longest x2 6.18 us: passed_along(): return lax.ppermute(block, axis, route)]
    unnamed x10 -> x3, local copies, waits for them, and re-layouts: 6.66 us -> 0.75 us
    reduce_sum x9 -> x0, other arithmetic: 3.37 us -> none  [the longest x2 1.51 us: window_corner(): amount = jnp.sum(jnp.where(chosen, sizes, 0))]
  transfers between devices with their start and end apart: 6 -> 0, of which waited for: 2 -> 0; matrix products, arithmetic and copies ran while one was open for 4% -> 0% of each run, Pallas kernels for 0% -> 0%
where the time goes in v1:
time: 80.2 us; the launch traced here: 80 us
  Pallas kernels  76.7 us (96%)
  local copies, waits for them, and re-layouts  2.68 us (3%)
    pallas_call x1, Pallas kernels, shards(): pl.pallas_call(functools.partial(kernel, steps), out_shape=(jax.ShapeDtyp...  76.7 us
    reshape x1, local copies, waits for them, and re-layouts, shards(): return (attended, grads.reshape(HEADS, 2, D))  1.93 us

profile of v1, /device:TPU:1, one launch (start us, length us, event | category | flops | bytes accessed | tf_op | source)
XLA Modules:
  0.0 80.0 jit_solution(939084391540036995)
XLA Ops:
  0.6 76.7 %attend_and_reduce.1 = (bf16[256,768]{1,0:T(8,128)(2,1)}, f32[12,6144]{1,0:T(8,128)}) custom-call(s32[4]{0:T(128)} %len_ref.1, s32[4]{0:T(128)} %own_ref.1, bf16[3,128,768]{2,1,0:T(8,128)(2,1)} %proj_ref.1, bf16[256,1536]{1,0:T(8,128)(2,1)} %cot_ref.1), custom_call_target="tpu_custom_call" | custom-call | tf_op jit(solution)/shard_map/attend_and_reduce/pallas_call | solution.py:469
  77.4 0.0 copy-start
  77.4 1.9 %reshape.7 = f32[6,2,6144]{2,1,0:T(2,128)} reshape(f32[12,6144]{1,0:T(8,128)} %get-tuple-element.5) | data formatting | bytes 589824 | tf_op jit(solution)/shard_map/reshape | solution.py:483
  79.3 0.0 copy-done
  79.3 0.7 copy.7
Async XLA Ops:
  77.4 1.9 %copy-start = (bf16[256,768]{1,0:T(8,128)(2,1)S(1)}, bf16[256,768]{1,0:T(8,128)(2,1)}, u32[]{:S(2)}) copy-start(bf16[256,768]{1,0:T(8,128)(2,1)} %get-tuple-element.8) | copy-start | bytes 1179652

commit v2 on v1

v2 whole, which is shorter than its diff:
```python
import functools

import jax
import jax.numpy as jnp
from jax import lax
from jax.experimental import pallas as pl
from jax.experimental.pallas import tpu as pltpu
from jax.sharding import PartitionSpec as P

MESH = pl.DeviceIdType.MESH
BF16 = jnp.bfloat16
F32 = jnp.float32
NX, NY, NZ = 4, 4, 8
HD = 128
HEADS = 6
PART = HEADS // 2
WIDTH = HEADS * HD
HALF = PART * HD
ROWS = 128
SPAN = 64
PACK = 256
IMGS = 4
GROUPS = 2 * NY * NZ
FEAT = 1536
CHUNK = 512
SHARE = 2 * PART * 2
STACK = SHARE * CHUNK // HD
D = 6144
RING = {"y": NY, "z": NZ}
BLOCK = {"y": NZ * SHARE, "z": NY * SHARE}
OTHER = {"y": "z", "z": "y"}

UNITS = [
    (0, 0, "y", 0), (0, 1, "z", 0), (0, 2, "y", 0), (1, 0, "y", 0), (3, 0, "z", 0), (1, 1, "y", 0),
    (3, 1, "z", 0), (1, 2, "y", 1), (3, 2, "z", 1), (2, 0, "y", 1), (2, 1, "y", 1), (2, 2, "y", 1),
]


def place():
    dp = lax.axis_index("dp")
    chip = dp // 2
    return chip // NZ, chip % NZ, dp % 2, lax.axis_index("mp")


def device(y, z, core, x):
    return ((y % NY * NZ + z % NZ) * 2 + core, x % NX)


def second_routes(u, units):
    _, _, first, direct = units[u]
    n = RING[OTHER[first]]
    routes = []
    if direct:
        for rel in sorted(range(1, n), key=lambda v: -min(v, n - v)):
            routes.append((rel, 0 if rel <= n // 2 else 1, min(rel, n - rel), rel, None))
        return routes, [route[0] for route in routes]
    for k in range(n // 2):
        for s in (0, 1):
            if k == 0 and s != u % 2:
                continue
            far = n // 2 - k
            adds = s * 4 + k - 1 if k > 1 or (k == 1 and s == u % 2) else None
            routes.append((s * 4 + k, s, 1, far if s == 0 else (n - far) % n, adds))
    return routes, [n // 2 - 1, 4 + n // 2 - 1]


def plan_steps(units, weights=(1.0, 0.0), detail=False):
    start = 9.5
    lat, hop, rate = 2.6, 0.6, 46e3
    done = {"B": start}
    links = {}
    tasks = {}

    def put(name, needs, spent, out=None):
        tasks[name] = (needs, spent, out)

    put(("X", 0), ["B"], 0.3, [
        ("outer", "z0", 1, 98304), ("p0", "x0", 1, 147456), ("p1", "x0", 1, 147456),
        ("m0", "x1", 1, 147456), ("m1", "x1", 1, 147456),
    ])
    put(("X", 1), ["outer"], 0.1, [("po", "x0", 1, 98304), ("mo", "x1", 1, 98304)])
    put(("X", 2), ["p0"], 0.1, [("f0", "x0", 1, 147456)])
    put(("X", 3), ["m1"], 0.1, [("f1", "x1", 1, 147456)])
    put(("X", 4), ["po", "mo", ("X", 2), ("X", 3)], 0.1, [("f2", "x0", 1, 49152), ("f3", "x1", 1, 49152)])
    feeds = {0: [("X", 1)], 1: ["m0", "m1", "mo"], 3: ["p0", "p1", "po"], 2: ["f0", "f1", "f2", "f3"]}
    for u, (r, fu, first, direct) in enumerate(units):
        h1, h2 = RING[first] // 2, RING[OTHER[first]] // 2
        size = BLOCK[first] * CHUNK * 2
        put(("M", u), feeds[r], 0.35)
        for k in range(h1):
            for s in (0, 1):
                needs = [("M", u)] + ([("R1", u, s, k - 1)] if k else [])
                sent = size // 2 if k == 0 else size
                put(("S1", u, s, k), needs, 0.1, [(("R1", u, s, k), first + str(s), 1, sent)])
        put(("F1", u), [("R1", u, 0, h1 - 1), ("R1", u, 1, h1 - 1)], 0.15)
        routes, ends = second_routes(u, units)
        for key, s, hops, _, adds in routes:
            needs = [("F1", u)] + ([("R2", u, adds)] if adds is not None else [])
            put(("S2", u, key), needs, 0.07, [(("R2", u, key), OTHER[first] + str(s), hops, 12288)])
        put(("F2", u), [("R2", u, key) for key in ends], 0.1, [(("O", u), "o", 1 + (r == 2), 32768)])
    depth = {"M": 0, "S1": 1, "F1": 6, "S2": 7, "F2": 12, "X": 50}

    def rank(name):
        level = depth[name[0]]
        if name[0] == "S1":
            level += name[3]
        if name[0] == "X":
            return (-100.0, name[1])
        return (weights[0] * name[1] + weights[1] * level, name[1], -level, name[2:])

    now = start
    order = []
    while tasks:
        best = None
        for name, (needs, _, _) in tasks.items():
            if all(n in done for n in needs):
                at = max(done[n] for n in needs)
                key = (0, 0.0) if at <= now else (1, at)
                if best is None or (key, rank(name)) < best[0]:
                    best = ((key, rank(name)), name, at)
        _, name, at = best
        _, spent, out = tasks.pop(name)
        now = max(now, at) + spent
        done[name] = now
        order.append(name)
        for label, link, hops, size in out or []:
            end = max(links.get(link, 0.0), now) + hops * size / rate
            links[link] = end
            done[label] = end + lat + hop * (hops - 1)
    if detail:
        return order, max(done.values()), done, links
    return order


def attend(len_ref, own_ref, proj_ref, group, core, att):
    lens = [len_ref[j] for j in range(IMGS)]
    ends = [lens[0], lens[0] + lens[1], lens[0] + lens[1] + lens[2]]
    starts = [jnp.int32(0)] + ends
    stops = ends + [ends[2] + lens[3]]
    row = lax.broadcasted_iota(jnp.int32, (ROWS, ROWS), 0)
    col = lax.broadcasted_iota(jnp.int32, (ROWS, ROWS), 1)

    def image(at):
        return sum((at >= e).astype(jnp.int32) for e in ends)

    same = image(row) == image(col)
    scale = HD ** (-0.5)

    def norm(values):
        values = values.astype(F32)
        centred = values - jnp.mean(values, axis=-1, keepdims=True)
        spread = jnp.mean(centred * centred, axis=-1, keepdims=True)
        return (centred * lax.rsqrt(spread + 1e-06)).astype(BF16)

    for h in range(HEADS):
        lanes = slice(h * HD, (h + 1) * HD)
        q = norm(proj_ref[0, :, lanes])
        k = norm(proj_ref[1, :, lanes])
        scores = lax.dot_general(q, k, (((1,), (1,)), ((), ())), preferred_element_type=F32) * scale
        raised = jnp.where(same, jnp.exp(scores), 0.0)
        totals = jnp.sum(raised, axis=-1, keepdims=True)
        weights = (raised / totals).astype(BF16)
        out = jnp.dot(weights, proj_ref[2, :, lanes], preferred_element_type=F32)
        att[:, lanes] = out.astype(BF16)

    stays = jnp.zeros((ROWS, ROWS), jnp.bool_)
    for j in range(IMGS):
        stays = stays | ((row >= starts[j]) & (row < stops[j]) & (own_ref[j] == group))
    picks = [jnp.where((row == col) & stays, 1.0, 0.0).astype(BF16)]
    row64 = lax.broadcasted_iota(jnp.int32, (SPAN, ROWS), 0)
    col64 = lax.broadcasted_iota(jnp.int32, (SPAN, ROWS), 1)
    for target in (group + 1 - 2 * core, group + GROUPS - 1 + 2 * core):
        first = jnp.int32(0)
        stop = jnp.int32(0)
        for j in range(IMGS):
            chosen = own_ref[j] == target % GROUPS
            first = first + jnp.where(chosen, starts[j], 0)
            stop = stop + jnp.where(chosen, stops[j], 0)
        corner = jnp.minimum(first, ROWS - SPAN)
        pick = (col64 == row64 + corner) & (col64 >= first) & (col64 < stop)
        picks.append(jnp.where(pick, 1.0, 0.0).astype(BF16))
    return picks


def order_matrix(y, z, first):
    i = lax.broadcasted_iota(jnp.int32, (HALF, HD), 0)
    lane = lax.broadcasted_iota(jnp.int32, (HALF, HD), 1)
    block = (i * 5462) >> 16
    inner = i - SHARE * block
    core = (inner >= SHARE // 2).astype(jnp.int32)
    inner = inner - (SHARE // 2) * core
    if first == "y":
        yd, zd = block >> 3, block
    else:
        yd, zd = block, block >> 2
    yd = (yd + y) & (NY - 1)
    zd = (zd + z) & (NZ - 1)
    d = ((yd * NZ + zd) * 2 + core) * 2 + (inner & 1)
    head = inner >> 1
    return [jnp.where((lane == d) & (head == h), 1.0, 0.0).astype(BF16) for h in range(PART)]


def kernel(
    steps, len_ref, own_ref, proj_ref, cot_ref, att_out, grad_out,
    att, outb, extra, cotb, gathered, order, turned, partial, sum1_out, sum1_in, sum2, sum2_out, sum2_in, final, grads,
    send_sem, recv_sem, local_sem,
):
    y, z, core, x = place()
    other = 1 - core
    chip = y * NZ + z
    group = chip * 2 + core
    after = (chip + 1) % (NY * NZ)
    before = (chip + NY * NZ - 1) % (NY * NZ)
    sibling = device(y, z, other, x)

    def shifted(axis, by, which=None):
        c = core if which is None else which
        if axis == "x":
            return device(y, z, c, x + by % NX)
        if axis == "y":
            return device(y + by % NY, z, c, x)
        return device(y, z + by % NZ, c, x)

    partners = [sibling]
    partners += [shifted("y", by) for by in range(1, NY)]
    partners += [shifted("z", by) for by in range(1, NZ)]
    partners += [shifted("x", by, which) for by in range(1, NX) for which in (0, 1)]
    partners += [(c * 2 + which, x) for c in (after, before) for which in (0, 1)]
    barrier = pltpu.get_barrier_semaphore()
    for p in partners:
        pl.semaphore_signal(barrier, inc=1, device_id=p, device_id_type=MESH)

    counter = [0]
    sent = []

    def message(src, dst, target):
        n = counter[0]
        counter[0] += 1
        copy = pltpu.make_async_remote_copy(
            src_ref=src, dst_ref=dst, send_sem=send_sem.at[n], recv_sem=recv_sem.at[n],
            device_id=target, device_id_type=MESH,
        )
        copy.start()
        sent.append(copy)
        return copy

    def rows(start, size):
        return pl.ds(pl.multiple_of(start, 64), size)

    mine = ROWS + SPAN
    own_rows = rows(core * mine, mine)
    outer_at = 2 * mine
    cot_pieces = [
        (pl.ds(0, ROWS), rows(core * mine, ROWS)),
        (pl.ds(ROWS, SPAN), rows(other * outer_at + core * ROWS, SPAN)),
        (pl.ds(ROWS + SPAN, SPAN), rows(other * (mine + ROWS) + core * (outer_at + SPAN), SPAN)),
    ]
    cot_here = []
    for n, (src, dst) in enumerate(cot_pieces):
        copy = pltpu.make_async_copy(cot_ref.at[src], cotb.at[dst], local_sem.at[n])
        copy.start()
        cot_here.append(copy)

    picks = attend(len_ref, own_ref, proj_ref, group, core, att)
    start = 0
    for pick in picks:
        part = jnp.dot(pick, att[...], preferred_element_type=F32).astype(BF16)
        for c in (0, 1):
            outb[c, start : start + pick.shape[0]] = part[:, c * HALF : (c + 1) * HALF]
        start += pick.shape[0]
    gathered[0, own_rows] = outb[core, 0:mine]
    for n, first in enumerate(("y", "z")):
        for h, piece in enumerate(order_matrix(y, z, first)):
            order[n, :, h * HD : (h + 1) * HD] = piece

    pl.semaphore_wait(barrier, len(partners))

    outer_chip = before * other + after * core
    outer_rows = [pl.ds(outer_at, SPAN), pl.ds(outer_at + SPAN, SPAN)]
    base = counter[0]
    counter[0] += 2
    outer_dst = rows(outer_at + SPAN * other, SPAN)
    for which in (0, 1):
        copy = pltpu.make_async_remote_copy(
            src_ref=outb.at[which, pl.ds(mine, SPAN)], dst_ref=gathered.at[0, outer_dst],
            send_sem=send_sem.at[base + which], recv_sem=recv_sem.at[base + core],
            device_id=(outer_chip * 2 + which, x), device_id_type=MESH,
        )
        copy.start()
        sent.append(copy)
    outer = [
        pltpu.make_async_remote_copy(
            src_ref=outb.at[0, pl.ds(mine, SPAN)], dst_ref=gathered.at[0, outer_rows[1 - which]],
            send_sem=send_sem.at[base + which], recv_sem=recv_sem.at[base + which],
            device_id=sibling, device_id_type=MESH,
        )
        for which in (0, 1)
    ]
    inner_cp = message(outb.at[other, pl.ds(0, mine)], gathered.at[0, own_rows], sibling)
    across = {}
    for slot, by in ((3, 1), (1, 3)):
        base = counter[0]
        counter[0] += 2
        for which in (0, 1):
            copy = pltpu.make_async_remote_copy(
                src_ref=outb.at[which, pl.ds(0, mine)], dst_ref=gathered.at[slot, own_rows],
                send_sem=send_sem.at[base + which], recv_sem=recv_sem.at[base + core],
                device_id=shifted("x", by, which), device_id_type=MESH,
            )
            copy.start()
            sent.append(copy)
            across[slot, which] = pltpu.make_async_remote_copy(
                src_ref=outb.at[0, pl.ds(0, mine)], dst_ref=gathered.at[slot, pl.ds(which * mine, mine)],
                send_sem=send_sem.at[base + which], recv_sem=recv_sem.at[base + which],
                device_id=sibling, device_id_type=MESH,
            )
    cot_there = [message(cot_ref.at[src], cotb.at[dst], sibling) for src, dst in cot_pieces]
    extra_inner = message(outb.at[core, pl.ds(ROWS, SPAN)], extra.at[0], sibling)

    waited = set()

    def arrived(copy):
        if id(copy) not in waited:
            waited.add(id(copy))
            copy.wait_recv()

    moved = {}

    def do_move(n):
        if n == 0:
            return
        if n == 1:
            for copy in outer:
                arrived(copy)
            both = pl.ds(outer_at, 2 * SPAN)
            moved["po"] = message(gathered.at[0, both], gathered.at[3, both], shifted("x", 1))
            moved["mo"] = message(gathered.at[0, both], gathered.at[1, both], shifted("x", 3))
            arrived(inner_cp)
            theirs = rows(outer_at + SPAN * other, SPAN)
            moved["extra"] = message(gathered.at[0, theirs], extra.at[1], sibling)
        elif n == 2:
            arrived(across[3, 0])
            part = pl.ds(0, mine)
            moved["f0"] = message(gathered.at[3, part], gathered.at[2, part], shifted("x", 1))
        elif n == 3:
            arrived(across[1, 1])
            part = pl.ds(mine, mine)
            moved["f1"] = message(gathered.at[1, part], gathered.at[2, part], shifted("x", 3))
        else:
            arrived(moved["po"])
            arrived(moved["mo"])
            moved["f2"] = message(gathered.at[3, outer_rows[0]], gathered.at[2, outer_rows[0]], shifted("x", 1))
            moved["f3"] = message(gathered.at[1, outer_rows[1]], gathered.at[2, outer_rows[1]], shifted("x", 3))

    turned_at = {}

    def turn(r, first):
        if (r, first) in turned_at:
            return turned_at[r, first]
        if r == 2:
            for label in ("f0", "f1", "f2", "f3"):
                arrived(moved[label])
        elif r:
            arrived(across[r, 0])
            arrived(across[r, 1])
            arrived(moved["po" if r == 3 else "mo"])
        n = len(turned_at)
        turned[n] = lax.dot_general(
            order["yz".index(first)], gathered[r], (((1,), (1,)), ((), ())), preferred_element_type=F32
        ).astype(BF16)
        turned_at[r, first] = n
        return n

    def do_multiply(u):
        r, fu, first, _ = UNITS[u]
        n = turn(r, first)
        if u == 0:
            for copy in cot_here:
                copy.wait()
            for copy in cot_there:
                arrived(copy)
        partial[u] = jnp.dot(turned[n], cotb[:, fu * CHUNK : (fu + 1) * CHUNK], preferred_element_type=F32)

    received = {}

    def do_first(u, s, k):
        first = UNITS[u][2]
        n, size = RING[first], BLOCK[first]
        far = n // 2 - k
        rel = far if s == 0 else (n - far) % n
        total = partial[u, rel * size : (rel + 1) * size]
        half = pl.ds(s * CHUNK // 2, CHUNK // 2) if k == 0 else pl.ds(0, CHUNK)
        spot = (u, s, pl.ds(k * size, size), half)
        if k == 0:
            total = total[:, s * CHUNK // 2 : (s + 1) * CHUNK // 2]
        else:
            received[1, u, s, k - 1].wait_recv()
            before_rows = pl.ds((k - 1) * size, size)
            if k == 1:
                got = sum1_in[u, s, before_rows, s * CHUNK // 2 : (s + 1) * CHUNK // 2].astype(F32)
                parts = [total[:, : CHUNK // 2], total[:, CHUNK // 2 :]]
                parts[s] = parts[s] + got
                total = jnp.concatenate(parts, axis=1)
            else:
                total = total + sum1_in[u, s, before_rows].astype(F32)
        sum1_out[spot] = total.astype(BF16)
        received[1, u, s, k] = message(
            sum1_out.at[spot], sum1_in.at[spot], shifted(first, 1 if s == 0 else n - 1)
        )

    def do_turn(u):
        first = UNITS[u][2]
        size, k = BLOCK[first], RING[first] // 2 - 1
        total = partial[u, 0:size]
        for s in (0, 1):
            received[1, u, s, k].wait_recv()
            total = total + sum1_in[u, s, pl.ds(k * size, size)].astype(F32)
        for b in range(RING[OTHER[first]]):
            block = total[b * SHARE : (b + 1) * SHARE]
            sum2[u, b] = jnp.concatenate([block[:, p * HD : (p + 1) * HD] for p in range(CHUNK // HD)], axis=0)

    def do_second(u, key):
        axis = OTHER[UNITS[u][2]]
        n = RING[axis]
        _, s, hops, rel, adds = next(route for route in second_routes(u, UNITS)[0] if route[0] == key)
        total = sum2[u, rel]
        if adds is not None:
            received[2, u, adds].wait_recv()
            total = total + sum2_in[u, adds].astype(F32)
        sum2_out[u, key] = total.astype(BF16)
        received[2, u, key] = message(
            sum2_out.at[u, key], sum2_in.at[u, key], shifted(axis, hops if s == 0 else n - hops)
        )

    arriving = []

    def do_last(u):
        r, fu, _, _ = UNITS[u]
        total = sum2[u, 0]
        for key in second_routes(u, UNITS)[1]:
            received[2, u, key].wait_recv()
            total = total + sum2_in[u, key].astype(F32)
        part = SHARE // 2
        for c in (0, 1):
            for p in range(CHUNK // HD):
                start = p * SHARE + c * part
                final[u, c, 0:part, p * HD : (p + 1) * HD] = total[start : start + part]
        here = pl.ds(pl.multiple_of(x * FEAT + fu * CHUNK, CHUNK), CHUNK)
        if r == 0:
            copy = pltpu.make_async_copy(final.at[u, core], grads.at[core, :, here], local_sem.at[3 + fu])
            copy.start()
            arriving.append((copy, True))
            arriving.append((message(final.at[u, other], grads.at[core, :, here], sibling), False))
            return
        base = counter[0]
        counter[0] += 2
        for which in (0, 1):
            copy = pltpu.make_async_remote_copy(
                src_ref=final.at[u, which], dst_ref=grads.at[core, :, here],
                send_sem=send_sem.at[base + which], recv_sem=recv_sem.at[base + core],
                device_id=shifted("x", r, which), device_id_type=MESH,
            )
            copy.start()
            sent.append(copy)
            there = pl.ds(pl.multiple_of((x + NX - r) % NX * FEAT + fu * CHUNK, CHUNK), CHUNK)
            wait = pltpu.make_async_remote_copy(
                src_ref=final.at[u, which], dst_ref=grads.at[which, :, there],
                send_sem=send_sem.at[base + which], recv_sem=recv_sem.at[base + which],
                device_id=sibling, device_id_type=MESH,
            )
            arriving.append((wait, False))

    run = {"X": do_move, "M": do_multiply, "S1": do_first, "F1": do_turn, "S2": do_second, "F2": do_last}
    for name in steps:
        run[name[0]](*name[1:])

    arrived(extra_inner)
    arrived(moved["extra"])
    att_out[0:ROWS, 0:HALF] = outb[0, 0:ROWS]
    att_out[0:ROWS, HALF:WIDTH] = outb[1, 0:ROWS]
    lanes = pl.ds(pl.multiple_of(core * HALF, HD), HALF)
    lanes_other = pl.ds(pl.multiple_of(other * HALF, HD), HALF)
    from_inner = rows(ROWS + SPAN * other, SPAN)
    from_outer = rows(ROWS + SPAN * core, SPAN)
    att_out[from_inner, lanes] = gathered[0, rows(other * mine + ROWS, SPAN)]
    att_out[from_inner, lanes_other] = extra[0]
    att_out[from_outer, lanes] = gathered[0, rows(outer_at + SPAN * core, SPAN)]
    att_out[from_outer, lanes_other] = extra[1]

    for copy, local in arriving:
        if local:
            copy.wait()
        else:
            copy.wait_recv()
    for h in range(HEADS):
        row = h % PART * 2
        grad_out[h] = grads[h // PART, row : row + 2]
    for copy in sent:
        copy.wait_send()


def shards(projected, lengths, owners, cotangent):
    steps = plan_steps(UNITS)
    units = len(UNITS)
    messages = 24 + 15 * units
    vmem = pl.BlockSpec(memory_space=pltpu.VMEM)
    smem = pl.BlockSpec(memory_space=pltpu.SMEM)
    scratch = [
        pltpu.VMEM((ROWS, WIDTH), BF16),
        pltpu.VMEM((2, PACK, HALF), BF16),
        pltpu.VMEM((2, SPAN, HALF), BF16),
        pltpu.VMEM((2 * PACK, FEAT), BF16),
        pltpu.VMEM((NX, 2 * PACK, HALF), BF16),
        pltpu.VMEM((2, HALF, HALF), BF16),
        pltpu.VMEM((2 * NX, HALF, 2 * PACK), BF16),
        pltpu.VMEM((units, HALF, CHUNK), F32),
        pltpu.VMEM((units, 2, HALF // 2, CHUNK), BF16),
        pltpu.VMEM((units, 2, HALF // 2, CHUNK), BF16),
        pltpu.VMEM((units, NZ, STACK, HD), F32),
        pltpu.VMEM((units, NZ, STACK, HD), BF16),
        pltpu.VMEM((units, NZ, STACK, HD), BF16),
        pltpu.VMEM((units, 2, 8, CHUNK), F32),
        pltpu.VMEM((2, 8, D), F32),
        pltpu.SemaphoreType.DMA((messages,)),
        pltpu.SemaphoreType.DMA((messages,)),
        pltpu.SemaphoreType.DMA((8,)),
    ]
    return pl.pallas_call(
        functools.partial(kernel, steps),
        out_shape=(
            jax.ShapeDtypeStruct((PACK, WIDTH), BF16),
            jax.ShapeDtypeStruct((HEADS, 2, D), F32),
        ),
        in_specs=[smem, smem, vmem, pl.BlockSpec(memory_space=pl.ANY)],
        out_specs=(vmem, vmem),
        scratch_shapes=scratch,
        compiler_params=pltpu.CompilerParams(
            collective_id=0, has_side_effects=True, vmem_limit_bytes=56 * 2**20
        ),
        name="attend_and_reduce",
    )(lengths, owners, projected, cotangent)


def solution(mesh):
    return jax.shard_map(
        shards,
        mesh=mesh,
        in_specs=(P(None, "dp", "mp"), P("dp"), P("dp"), P("dp", "mp")),
        out_specs=(P("dp", "mp"), P("mp", "dp", None)),
        check_vma=False,
    )
```

time: 80.2 us -> 65.1 us (0.81)
  Pallas kernels: 76.7 us -> 61.9 us
    pallas_call x1, Pallas kernels: 76.7 us -> 61.9 us  [shards(): pl.pallas_call(functools.partial(kernel, steps), out_shape=(jax.ShapeDtyp...]
    reshape x1 -> x0, local copies, waits for them, and re-layouts: 1.93 us -> none  [shards(): return (attended, grads.reshape(HEADS, 2, D))]
    unnamed x3 -> x4, local copies, waits for them, and re-layouts: 0.75 us -> 2.53 us
where the time goes in v2:
time: 65.1 us; the launch traced here: 65 us
  Pallas kernels  61.9 us (95%)
  local copies, waits for them, and re-layouts  2.53 us (4%)
    pallas_call x1, Pallas kernels, shards(): pl.pallas_call(functools.partial(kernel, steps), out_shape=(jax.ShapeDtyp...  61.9 us
    unnamed x4, local copies, waits for them, and re-layouts  2.53 us

profile of v2, /device:TPU:1, one launch (start us, length us, event | category | flops | bytes accessed | tf_op | source)
XLA Modules:
  0.0 65.0 jit_solution(15148078476777202394)
XLA Ops:
  0.6 61.9 %attend_and_reduce.1 = (bf16[256,768]{1,0:T(8,128)(2,1)}, f32[6,2,6144]{2,1,0:T(2,128)}) custom-call(s32[4]{0:T(128)} %len_ref.1, s32[4]{0:T(128)} %own_ref.1, bf16[3,128,768]{2,1,0:T(8,128)(2,1)} %proj_ref.1, bf16[256,1536]{1,0:T(8,128)(2,1)} %cot_ref.1), custom_call_target="tpu_custom_call" | custom-call | tf_op jit(solution)/shard_map/attend_and_reduce/pallas_call | solution.py:528
  62.5 0.0 copy-start
  62.5 1.8 %copy.8 = bf16[256,768]{1,0:T(8,128)(2,1)} copy(bf16[256,768]{1,0:T(8,128)(2,1)} %get-tuple-element.4) | data formatting | bytes 786432
  64.3 0.0 copy-done
  64.3 0.7 %copy.9 = f32[6,2,6144]{2,1,0:T(2,128)} copy(f32[6,2,6144]{2,1,0:T(2,128)S(1)} %copy-done) | data formatting | bytes 589824
Async XLA Ops:
  62.5 1.8 %copy-start = (f32[6,2,6144]{2,1,0:T(2,128)S(1)}, f32[6,2,6144]{2,1,0:T(2,128)}, u32[]{:S(2)}) copy-start(f32[6,2,6144]{2,1,0:T(2,128)} %get-tuple-element.5) | copy-start | bytes 884740

commit v3 on v2

v3 whole, which is shorter than its diff:
```python
import functools

import jax
import jax.numpy as jnp
from jax import lax
from jax.experimental import pallas as pl
from jax.experimental.pallas import tpu as pltpu
from jax.sharding import PartitionSpec as P

MESH = pl.DeviceIdType.MESH
BF16 = jnp.bfloat16
F32 = jnp.float32
NX, NY, NZ = 4, 4, 8
HD = 128
HEADS = 6
PART = HEADS // 2
WIDTH = HEADS * HD
HALF = PART * HD
ROWS = 128
SPAN = 64
PACK = 256
IMGS = 4
GROUPS = 2 * NY * NZ
FEAT = 1536
SHARE = 2 * 2
STACK = SHARE * FEAT // HD
D = 6144
RING = {"y": NY, "z": NZ}
BLOCK = {"y": NZ * SHARE, "z": NY * SHARE}
OTHER = {"y": "z", "z": "y"}

UNITS = [
    (0, 0, "y", 0), (0, 1, "z", 1), (0, 2, "y", 0), (1, 0, "y", 0), (3, 0, "z", 1), (1, 1, "y", 0),
    (3, 1, "z", 1), (1, 2, "y", 1), (3, 2, "z", 1), (2, 0, "y", 1), (2, 1, "y", 1), (2, 2, "y", 1),
]
EARLY = 2
SENDING = 64


def place():
    dp = lax.axis_index("dp")
    chip = dp // 2
    return chip // NZ, chip % NZ, dp % 2, lax.axis_index("mp")


def device(y, z, core, x):
    return ((y % NY * NZ + z % NZ) * 2 + core, x % NX)


def second_routes(u, units):
    _, _, first, direct = units[u]
    n = RING[OTHER[first]]
    routes = []
    if direct:
        for rel in sorted(range(1, n), key=lambda v: -min(v, n - v)):
            routes.append((rel, 0 if rel <= n // 2 else 1, min(rel, n - rel), rel, None))
        return routes, [route[0] for route in routes]
    for k in range(n // 2):
        for s in (0, 1):
            if k == 0 and s != u % 2:
                continue
            far = n // 2 - k
            adds = s * 4 + k - 1 if k > 1 or (k == 1 and s == u % 2) else None
            routes.append((s * 4 + k, s, 1, far if s == 0 else (n - far) % n, adds))
    return routes, [n // 2 - 1, 4 + n // 2 - 1]


def plan_steps(units, weights=(1.0, 0.0), detail=False):
    start = 9.5
    lat, hop, rate = 2.6, 0.6, 46e3
    done = {"B": start}
    links = {}
    tasks = {}

    def put(name, needs, spent, out=None):
        tasks[name] = (needs, spent, out)

    early, late = 49152 * EARLY, 49152 * (PART - EARLY)
    put(("X", 0), ["B"], 0.3, [
        ("outer", "z0", 1, 49152), ("p0", "x0", 1, early), ("p1", "x0", 1, early),
        ("m0", "x1", 1, early), ("m1", "x1", 1, early),
    ])
    put(("X", 1), ["outer"], 0.2, [
        ("po", "x0", 1, 98304), ("mo", "x1", 1, 98304), ("p2", "x0", 1, late), ("p3", "x0", 1, late),
        ("m2", "x1", 1, late), ("m3", "x1", 1, late),
    ])
    put(("X", 2), ["p0"], 0.1, [("f0", "x0", 1, early)])
    put(("X", 3), ["m1"], 0.1, [("f1", "x1", 1, early)])
    put(("X", 4), ["po", "mo", ("X", 2), ("X", 3)], 0.1, [("f2", "x0", 1, 49152), ("f3", "x1", 1, 49152)])
    put(("X", 6), ["f0"], 0.2, None)
    put(("X", 5), ["p2", "m3", ("X", 4)], 0.1, [("f4", "x0", 1, late), ("f5", "x1", 1, late)])
    feeds = {0: [("X", 1)], 1: ["m0", "m1", "mo"], 3: ["p0", "p1", "po"], 2: ["f0", "f1", "f2", "f3"]}
    rest = {0: [], 1: ["m2", "m3"], 3: ["p2", "p3"], 2: ["f4", "f5"]}
    for u, (r, h, first, direct) in enumerate(units):
        h1, h2 = RING[first] // 2, RING[OTHER[first]] // 2
        size = BLOCK[first] * FEAT * 2
        put(("M", u), feeds[r] + (rest[r] if h >= EARLY else []), 0.45)
        for k in range(h1):
            for s in (0, 1):
                needs = [("M", u)] + ([("R1", u, s, k - 1)] if k else [])
                sent = size // 2 if k == 0 else size
                put(("S1", u, s, k), needs, 0.1, [(("R1", u, s, k), first + str(s), 1, sent)])
        put(("F1", u), [("R1", u, 0, h1 - 1), ("R1", u, 1, h1 - 1)], 0.15)
        routes, ends = second_routes(u, units)
        for key, s, hops, _, adds in routes:
            needs = [("F1", u)] + ([("R2", u, adds)] if adds is not None else [])
            put(("S2", u, key), needs, 0.07, [(("R2", u, key), OTHER[first] + str(s), hops, 12288)])
        put(("F2", u), [("R2", u, key) for key in ends], 0.1, [(("O", u), "o" + str(r), 1 + (r == 2) - 2.5 * (r == 0), 12288)])
    depth = {"M": 0, "S1": 1, "F1": 6, "S2": 7, "F2": 12, "X": 50}

    def rank(name):
        level = depth[name[0]]
        if name[0] == "S1":
            level += name[3]
        if name[0] == "X":
            return (-100.0, name[1])
        return (weights[0] * name[1] + weights[1] * level, name[1], -level, name[2:])

    now = start
    order = []
    while tasks:
        best = None
        for name, (needs, _, _) in tasks.items():
            if all(n in done for n in needs):
                at = max(done[n] for n in needs)
                key = (0, 0.0) if at <= now else (1, at)
                if best is None or (key, rank(name)) < best[0]:
                    best = ((key, rank(name)), name, at)
        _, name, at = best
        _, spent, out = tasks.pop(name)
        now = max(now, at) + spent
        done[name] = now
        order.append(name)
        for label, link, hops, size in out or []:
            end = max(links.get(link, 0.0), now) + max(hops, 1) * size / rate
            links[link] = end
            done[label] = end + lat + hop * (hops - 1)
    if detail:
        return order, max(done.values()), done, links
    return order


def attend(len_ref, own_ref, proj_ref, group, core, att):
    lens = [len_ref[j] for j in range(IMGS)]
    ends = [lens[0], lens[0] + lens[1], lens[0] + lens[1] + lens[2]]
    starts = [jnp.int32(0)] + ends
    stops = ends + [ends[2] + lens[3]]
    row = lax.broadcasted_iota(jnp.int32, (ROWS, ROWS), 0)
    col = lax.broadcasted_iota(jnp.int32, (ROWS, ROWS), 1)

    def image(at):
        return sum((at >= e).astype(jnp.int32) for e in ends)

    same = image(row) == image(col)
    scale = HD ** (-0.5)

    def norm(values):
        values = values.astype(F32)
        centred = values - jnp.mean(values, axis=-1, keepdims=True)
        spread = jnp.mean(centred * centred, axis=-1, keepdims=True)
        return (centred * lax.rsqrt(spread + 1e-06)).astype(BF16)

    for h in range(HEADS):
        lanes = slice(h * HD, (h + 1) * HD)
        q = norm(proj_ref[0, :, lanes])
        k = norm(proj_ref[1, :, lanes])
        scores = lax.dot_general(q, k, (((1,), (1,)), ((), ())), preferred_element_type=F32) * scale
        raised = jnp.where(same, jnp.exp(scores), 0.0)
        totals = jnp.sum(raised, axis=-1, keepdims=True)
        weights = (raised / totals).astype(BF16)
        out = jnp.dot(weights, proj_ref[2, :, lanes], preferred_element_type=F32)
        att[:, lanes] = out.astype(BF16)

    stays = jnp.zeros((ROWS, ROWS), jnp.bool_)
    for j in range(IMGS):
        stays = stays | ((row >= starts[j]) & (row < stops[j]) & (own_ref[j] == group))
    picks = [jnp.where((row == col) & stays, 1.0, 0.0).astype(BF16)]
    row64 = lax.broadcasted_iota(jnp.int32, (SPAN, ROWS), 0)
    col64 = lax.broadcasted_iota(jnp.int32, (SPAN, ROWS), 1)
    for target in (group + 1 - 2 * core, group + GROUPS - 1 + 2 * core):
        first = jnp.int32(0)
        stop = jnp.int32(0)
        for j in range(IMGS):
            chosen = own_ref[j] == target % GROUPS
            first = first + jnp.where(chosen, starts[j], 0)
            stop = stop + jnp.where(chosen, stops[j], 0)
        corner = jnp.minimum(first, ROWS - SPAN)
        pick = (col64 == row64 + corner) & (col64 >= first) & (col64 < stop)
        picks.append(jnp.where(pick, 1.0, 0.0).astype(BF16))
    return picks


def order_matrix(y, z, first):
    i = lax.broadcasted_iota(jnp.int32, (HD, HD), 0)
    lane = lax.broadcasted_iota(jnp.int32, (HD, HD), 1)
    block = i >> 2
    if first == "y":
        yd, zd = block >> 3, block
    else:
        yd, zd = block, block >> 2
    yd = (yd + y) & (NY - 1)
    zd = (zd + z) & (NZ - 1)
    d = (yd * NZ + zd) * SHARE + (i & 3)
    return jnp.where(lane == d, 1.0, 0.0).astype(BF16)


def kernel(
    steps, len_ref, own_ref, proj_hbm, cot_ref, att_out, grad_out,
    proj_ref, att, att_all, outb, extra, cotb, gathered, order, partial, sum1_out, sum1_in, sum2, sum2_out, sum2_in, final, result,
    send_sem, recv_sem, local_sem,
):
    y, z, core, x = place()
    other = 1 - core
    chip = y * NZ + z
    group = chip * 2 + core
    after = (chip + 1) % (NY * NZ)
    before = (chip + NY * NZ - 1) % (NY * NZ)
    sibling = device(y, z, other, x)

    def shifted(axis, by, which=None):
        c = core if which is None else which
        if axis == "x":
            return device(y, z, c, x + by % NX)
        if axis == "y":
            return device(y + by % NY, z, c, x)
        return device(y, z + by % NZ, c, x)

    partners = [sibling]
    partners += [shifted("y", by) for by in range(1, NY)]
    partners += [shifted("z", by) for by in range(1, NZ)]
    partners += [shifted("x", by, which) for by in range(1, NX) for which in (0, 1)]
    partners += [(c * 2 + which, x) for c in (after, before) for which in (0, 1)]
    barrier = pltpu.get_barrier_semaphore()
    for p in partners:
        pl.semaphore_signal(barrier, inc=1, device_id=p, device_id_type=MESH)

    loads = []
    for n in range(3):
        copy = pltpu.make_async_copy(proj_hbm.at[n], proj_ref.at[n], local_sem.at[3 + n])
        copy.start()
        loads.append(copy)

    pool = send_sem.shape[0]
    counter = [0]
    sent = []

    def slot_for_send():
        if len(sent) >= pool:
            sent[len(sent) - pool].wait_send()
        return send_sem.at[len(sent) % pool]

    def fresh():
        counter[0] += 1
        return counter[0] - 1

    def message(src, dst, target, n=None):
        copy = pltpu.make_async_remote_copy(
            src_ref=src, dst_ref=dst, send_sem=slot_for_send(), recv_sem=recv_sem.at[fresh() if n is None else n],
            device_id=target, device_id_type=MESH,
        )
        copy.start()
        sent.append(copy)
        return copy

    def landing(dst, n):
        return pltpu.make_async_remote_copy(
            src_ref=dst, dst_ref=dst, send_sem=send_sem.at[0], recv_sem=recv_sem.at[n],
            device_id=sibling, device_id_type=MESH,
        )

    def rows(start, size):
        return pl.ds(pl.multiple_of(start, 64), size)

    mine = ROWS + SPAN
    own_rows = rows(core * mine, mine)
    outer_at = 2 * mine
    cot_pieces = [
        (pl.ds(0, ROWS), rows(core * mine, ROWS)),
        (pl.ds(ROWS, SPAN), rows(other * outer_at + core * ROWS, SPAN)),
        (pl.ds(ROWS + SPAN, SPAN), rows(other * (mine + ROWS) + core * (outer_at + SPAN), SPAN)),
    ]
    cot_here = []
    for n, (src, dst) in enumerate(cot_pieces):
        copy = pltpu.make_async_copy(cot_ref.at[src], cotb.at[dst], local_sem.at[n])
        copy.start()
        cot_here.append(copy)

    for copy in loads:
        copy.wait()
    picks = attend(len_ref, own_ref, proj_ref, group, core, att)
    start = 0
    for pick in picks:
        part = jnp.dot(pick, att[...], preferred_element_type=F32).astype(BF16)
        for h in range(HEADS):
            outb[h // PART, h % PART, start : start + pick.shape[0]] = part[:, h * HD : (h + 1) * HD]
        start += pick.shape[0]
    for h in range(PART):
        gathered[0, h, own_rows] = outb[core, h, 0:mine]
    for n, first in enumerate(("y", "z")):
        order[n] = order_matrix(y, z, first)

    pl.semaphore_wait(barrier, len(partners))

    outer_chip = before * other + after * core
    outer_rows = [pl.ds(outer_at, SPAN), pl.ds(outer_at + SPAN, SPAN)]
    every = pl.ds(0, PART)
    first_heads = pl.ds(0, EARLY)
    last_heads = pl.ds(EARLY, PART - EARLY)

    def crossing(sends, lands):
        base = fresh()
        fresh()
        for which in (0, 1):
            message(*sends(which), base + core)
        return [landing(lands(which), base + which) for which in (0, 1)]

    outer_dst = rows(outer_at + SPAN * other, SPAN)
    outer = crossing(
        lambda which: (
            outb.at[which, every, pl.ds(mine, SPAN)], gathered.at[0, every, outer_dst], (outer_chip * 2 + which, x)
        ),
        lambda which: gathered.at[0, every, outer_rows[1 - which]],
    )
    inner_cp = message(outb.at[other, every, pl.ds(0, mine)], gathered.at[0, every, own_rows], sibling)
    cot_there = [message(cot_ref.at[src], cotb.at[dst], sibling) for src, dst in cot_pieces]

    def send_across(heads):
        return {
            slot: crossing(
                lambda which: (
                    outb.at[which, heads, pl.ds(0, mine)], gathered.at[slot, heads, own_rows],
                    shifted("x", by, which),
                ),
                lambda which: gathered.at[slot, heads, pl.ds(which * mine, mine)],
            )
            for slot, by in ((3, 1), (1, 3))
        }

    across = {0: send_across(first_heads)}
    extra_inner = message(outb.at[core, every, pl.ds(ROWS, SPAN)], extra.at[0], sibling)

    waited = set()
    leaving = []

    def arrived(copy):
        if id(copy) not in waited:
            waited.add(id(copy))
            copy.wait_recv()

    moved = {}

    def forward(label, slot, heads, part):
        by = 1 if slot == 3 else 3
        moved[label] = message(gathered.at[slot, heads, part], gathered.at[2, heads, part], shifted("x", by))

    def write_attended():
        arrived(extra_inner)
        arrived(moved["extra"])
        from_inner = rows(ROWS + SPAN * other, SPAN)
        from_outer = rows(ROWS + SPAN * core, SPAN)
        for h in range(HEADS):
            att_all[0:ROWS, h * HD : (h + 1) * HD] = outb[h // PART, h % PART, 0:ROWS]
        for h in range(PART):
            here = pl.ds(pl.multiple_of(core * HALF + h * HD, HD), HD)
            there = pl.ds(pl.multiple_of(other * HALF + h * HD, HD), HD)
            att_all[from_inner, here] = gathered[0, h, rows(other * mine + ROWS, SPAN)]
            att_all[from_inner, there] = extra[0, h]
            att_all[from_outer, here] = gathered[0, h, rows(outer_at + SPAN * core, SPAN)]
            att_all[from_outer, there] = extra[1, h]
        copy = pltpu.make_async_copy(att_all, att_out, local_sem.at[6])
        copy.start()
        leaving.append(copy)

    def do_move(n):
        if n == 6:
            write_attended()
        elif n == 1:
            for copy in outer:
                arrived(copy)
            both = pl.ds(outer_at, 2 * SPAN)
            moved["po"] = message(gathered.at[0, every, both], gathered.at[3, every, both], shifted("x", 1))
            moved["mo"] = message(gathered.at[0, every, both], gathered.at[1, every, both], shifted("x", 3))
            across[1] = send_across(last_heads)
            arrived(inner_cp)
            theirs = rows(outer_at + SPAN * other, SPAN)
            moved["extra"] = message(gathered.at[0, every, theirs], extra.at[1], sibling)
        elif n == 2:
            arrived(across[0][3][0])
            forward("f0", 3, first_heads, pl.ds(0, mine))
        elif n == 3:
            arrived(across[0][1][1])
            forward("f1", 1, first_heads, pl.ds(mine, mine))
        elif n == 4:
            arrived(moved["po"])
            arrived(moved["mo"])
            forward("f2", 3, every, outer_rows[0])
            forward("f3", 1, every, outer_rows[1])
        elif n == 5:
            arrived(across[1][3][0])
            arrived(across[1][1][1])
            forward("f4", 3, last_heads, pl.ds(0, mine))
            forward("f5", 1, last_heads, pl.ds(mine, mine))

    def do_multiply(u):
        r, h, first, _ = UNITS[u]
        if r == 2:
            for label in ("f0", "f1", "f2", "f3") + (("f4", "f5") if h >= EARLY else ()):
                arrived(moved[label])
        elif r:
            for copy in across[0][r] + (across[1][r] if h >= EARLY else []):
                arrived(copy)
            arrived(moved["po" if r == 3 else "mo"])
        turned = lax.dot_general(
            order["yz".index(first)], gathered[r, h], (((1,), (1,)), ((), ())), preferred_element_type=F32
        ).astype(BF16)
        while cot_here:
            cot_here.pop().wait()
        for copy in cot_there:
            arrived(copy)
        partial[u] = jnp.dot(turned, cotb[...], preferred_element_type=F32)

    received = {}
    shared = {}

    def do_first(u, s, k):
        first = UNITS[u][2]
        n, size = RING[first], BLOCK[first]
        far = n // 2 - k
        rel = far if s == 0 else (n - far) % n
        total = partial[u, rel * size : (rel + 1) * size]
        half = pl.ds(s * FEAT // 2, FEAT // 2) if k == 0 else pl.ds(0, FEAT)
        spot = (u, s, pl.ds(k * size, size), half)
        if k == 0:
            total = total[:, s * FEAT // 2 : (s + 1) * FEAT // 2]
        else:
            received[1, u, s, k - 1].wait_recv()
            before_rows = pl.ds((k - 1) * size, size)
            if k == 1:
                got = sum1_in[u, s, before_rows, s * FEAT // 2 : (s + 1) * FEAT // 2].astype(F32)
                parts = [total[:, : FEAT // 2], total[:, FEAT // 2 :]]
                parts[s] = parts[s] + got
                total = jnp.concatenate(parts, axis=1)
            else:
                total = total + sum1_in[u, s, before_rows].astype(F32)
        sum1_out[spot] = total.astype(BF16)
        last = None
        if k == n // 2 - 1:
            last = shared.setdefault((1, u), -1)
            if last < 0:
                last = shared[1, u] = fresh()
        received[1, u, s, k] = message(
            sum1_out.at[spot], sum1_in.at[spot], shifted(first, 1 if s == 0 else n - 1), last
        )

    def do_turn(u):
        first = UNITS[u][2]
        size, k = BLOCK[first], RING[first] // 2 - 1
        total = partial[u, 0:size]
        landing(sum1_in.at[u, :, pl.ds(k * size, size)], shared[1, u]).wait_recv()
        for s in (0, 1):
            total = total + sum1_in[u, s, pl.ds(k * size, size)].astype(F32)
        for b in range(RING[OTHER[first]]):
            block = total[b * SHARE : (b + 1) * SHARE]
            pieces = [block[:, p * HD : (p + 1) * HD] for p in range(FEAT // HD)]
            sum2[u, b] = jnp.concatenate([p[2 * c : 2 * c + 2] for c in (0, 1) for p in pieces], axis=0)

    def do_second(u, key):
        axis = OTHER[UNITS[u][2]]
        n = RING[axis]
        _, s, hops, rel, adds = next(route for route in second_routes(u, UNITS)[0] if route[0] == key)
        total = sum2[u, rel]
        if adds is not None:
            received[2, u, adds].wait_recv()
            total = total + sum2_in[u, adds].astype(F32)
        sum2_out[u, key] = total.astype(BF16)
        one = None
        if UNITS[u][3]:
            one = shared.setdefault((2, u), -1)
            if one < 0:
                one = shared[2, u] = fresh()
        received[2, u, key] = message(
            sum2_out.at[u, key], sum2_in.at[u, key], shifted(axis, hops if s == 0 else n - hops), one
        )

    arriving = []

    def result_rows(u, source):
        return pl.ds(pl.multiple_of((UNITS[u][1] * NX + source) * (STACK // 2), 8), STACK // 2)

    def do_last(u):
        r = UNITS[u][0]
        total = sum2[u, 0]
        ends = second_routes(u, UNITS)[1]
        if UNITS[u][3]:
            landing(sum2_in.at[u, pl.ds(1, len(ends))], shared[2, u]).wait_recv()
        else:
            for key in ends:
                received[2, u, key].wait_recv()
        for key in ends:
            total = total + sum2_in[u, key].astype(F32)
        final[u, 0] = total[: STACK // 2]
        final[u, 1] = total[STACK // 2 :]
        here = result_rows(u, x)
        if r == 0:
            result[core, here] = final[u, core]
            copy = message(final.at[u, other], result.at[core, here], sibling)
            arriving.append((copy, here))
            return
        n = fresh()
        there = result_rows(u, (x + NX - r) % NX)
        for which in (0, 1):
            message(final.at[u, which], result.at[core, here], shifted("x", r, which), n)
        arriving.append((landing(result.at[:, there], n), there))

    run = {"X": do_move, "M": do_multiply, "S1": do_first, "F1": do_turn, "S2": do_second, "F2": do_last}
    for name in steps:
        run[name[0]](*name[1:])

    for copy, spot in arriving:
        copy.wait_recv()
        pltpu.make_async_copy(result.at[:, spot], grad_out.at[:, spot], local_sem.at[7]).start()
    pltpu.make_async_copy(result, grad_out, local_sem.at[7]).wait()
    for copy in leaving:
        copy.wait()
    assert counter[0] == recv_sem.shape[0]
    for copy in sent[-pool:]:
        copy.wait_send()


def receive_count(units):
    count = 24
    for u, (_, _, first, direct) in enumerate(units):
        count += RING[first] - 1 + (1 if direct else len(second_routes(u, units)[0])) + 1
    return count


def hand_over(attended_in, grads_in, attended_out, grads_out):
    attended_out[...] = attended_in[...]
    grads_out[...] = grads_in[...]


def shards(projected, lengths, owners, cotangent):
    steps = plan_steps(UNITS)
    units = len(UNITS)
    messages = receive_count(UNITS)
    vmem = pl.BlockSpec(memory_space=pltpu.VMEM)
    smem = pl.BlockSpec(memory_space=pltpu.SMEM)
    anywhere = pl.BlockSpec(memory_space=pl.ANY)
    scratch = [
        pltpu.VMEM((3, ROWS, WIDTH), BF16),
        pltpu.VMEM((ROWS, WIDTH), BF16),
        pltpu.VMEM((PACK, WIDTH), BF16),
        pltpu.VMEM((2, PART, PACK, HD), BF16),
        pltpu.VMEM((2, PART, SPAN, HD), BF16),
        pltpu.VMEM((2 * PACK, FEAT), BF16),
        pltpu.VMEM((NX, PART, 2 * PACK, HD), BF16),
        pltpu.VMEM((2, HD, HD), BF16),
        pltpu.VMEM((units, HD, FEAT), F32),
        pltpu.VMEM((units, 2, HD // 2, FEAT), BF16),
        pltpu.VMEM((units, 2, HD // 2, FEAT), BF16),
        pltpu.VMEM((units, NZ, STACK, HD), F32),
        pltpu.VMEM((units, NZ, STACK, HD), BF16),
        pltpu.VMEM((units, NZ, STACK, HD), BF16),
        pltpu.VMEM((units, 2, STACK // 2, HD), F32),
        pltpu.VMEM((2, HEADS * D // HD, HD), F32),
        pltpu.SemaphoreType.DMA((SENDING,)),
        pltpu.SemaphoreType.DMA((messages,)),
        pltpu.SemaphoreType.DMA((8,)),
    ]
    attended, grads = pl.pallas_call(
        functools.partial(kernel, steps),
        out_shape=(
            jax.ShapeDtypeStruct((PACK, WIDTH), BF16),
            jax.ShapeDtypeStruct((2, HEADS * D // HD, HD), F32),
        ),
        in_specs=[smem, smem, anywhere, anywhere],
        out_specs=(anywhere, anywhere),
        scratch_shapes=scratch,
        compiler_params=pltpu.CompilerParams(
            collective_id=0, has_side_effects=True, vmem_limit_bytes=60 * 2**20
        ),
        name="attend_and_reduce",
    )(lengths, owners, projected, cotangent)
    attended, grads = pl.pallas_call(
        hand_over,
        out_shape=(
            jax.ShapeDtypeStruct(attended.shape, BF16),
            jax.ShapeDtypeStruct(grads.shape, F32),
        ),
        in_specs=[vmem, vmem],
        out_specs=(vmem, vmem),
        name="hand_over",
    )(attended, grads)
    grads = grads.reshape(HEADS, D // HD, 2, HD).transpose(0, 2, 1, 3).reshape(HEADS, 2, D)
    return attended, grads


def solution(mesh):
    return jax.shard_map(
        shards,
        mesh=mesh,
        in_specs=(P(None, "dp", "mp"), P("dp"), P("dp"), P("dp", "mp")),
        out_specs=(P("dp", "mp"), P("mp", "dp", None)),
        check_vma=False,
    )
```

time: 65.1 us -> 60.7 us (0.932)
  local copies, waits for them, and re-layouts: 2.53 us -> 0 us
  Pallas kernels: 61.9 us -> 59.9 us
    pallas_call x1, Pallas kernels: 61.9 us -> 57.9 us  [shards(): pl.pallas_call(functools.partial(kernel, steps), out_shape=(jax.ShapeDtyp...]
    unnamed x4 -> x0, local copies, waits for them, and re-layouts: 2.53 us -> none
    pallas_call x0 -> x1, Pallas kernels: none -> 1.95 us  [shards(): pl.pallas_call(hand_over, out_shape=(jax.ShapeDtypeStruct(attended.shape,...]
where the time goes in v3:
time: 60.7 us; the launch traced here: 60.5 us
  Pallas kernels  59.9 us (99%)
  between operations  0.64 us (1%)
    pallas_call x1, Pallas kernels, shards(): pl.pallas_call(functools.partial(kernel, steps), out_shape=(jax.ShapeDtyp...  57.9 us
    pallas_call x1, Pallas kernels, shards(): pl.pallas_call(hand_over, out_shape=(jax.ShapeDtypeStruct(attended.shape,...  1.95 us

profile of v3, /device:TPU:1, one launch (start us, length us, event | category | flops | bytes accessed | tf_op | source)
XLA Modules:
  0.0 60.5 jit_solution(9519998126143527642)
XLA Ops:
  0.6 57.9 %attend_and_reduce.1 = (bf16[256,768]{1,0:T(8,128)(2,1)}, f32[2,288,128]{2,1,0:T(8,128)}) custom-call(s32[4]{0:T(128)} %len_ref.1, s32[4]{0:T(128)} %own_ref.1, bf16[3,128,768]{2,1,0:T(8,128)(2,1)} %proj_hbm.1, bf16[256,1536]{1,0:T(8,128)(2,1)} %cot_ref.1), custom_call_target="tpu_custom_call" | custom-call | tf_op jit(solution)/shard_map/attend_and_reduce/pallas_call | solution.py:570
  58.6 2.0 %hand_over.1 = (bf16[256,768]{1,0:T(8,128)(2,1)}, f32[2,288,128]{2,1,0:T(8,128)}) custom-call(bf16[256,768]{1,0:T(8,128)(2,1)} %get-tuple-element.6.attended_in, f32[2,288,128]{2,1,0:T(8,128)} %get-tuple-element.7.grads_in), custom_call_target="tpu_custom_call" | custom-call | tf_op jit(solution)/shard_map/hand_over/pallas_call | solution.py:584

commit v4 on v3

--- a/solution.py
+++ b/solution.py
@@ -30,10 +30,9 @@
 OTHER = {"y": "z", "z": "y"}
 
 UNITS = [
-    (0, 0, "y", 0), (0, 1, "z", 1), (0, 2, "y", 0), (1, 0, "y", 0), (3, 0, "z", 1), (1, 1, "y", 0),
-    (3, 1, "z", 1), (1, 2, "y", 1), (3, 2, "z", 1), (2, 0, "y", 1), (2, 1, "y", 1), (2, 2, "y", 1),
+    (2, 2, "y", 1), (0, 0, "y", 0), (2, 1, "z", 1), (1, 2, "y", 0), (1, 1, "z", 0), (3, 0, "y", 0),
+    (0, 2, "z", 1), (3, 1, "y", 0), (2, 0, "z", 1), (0, 1, "y", 0), (1, 0, "z", 0), (3, 2, "y", 1),
 ]
-EARLY = 2
 SENDING = 64
 
 
@@ -67,7 +66,7 @@
 
 def plan_steps(units, weights=(1.0, 0.0), detail=False):
     start = 9.5
-    lat, hop, rate = 2.6, 0.6, 46e3
+    lat, hop, rate = 2.6, 0.5, 54e3
     done = {"B": start}
     links = {}
     tasks = {}
@@ -75,32 +74,27 @@
     def put(name, needs, spent, out=None):
         tasks[name] = (needs, spent, out)
 
-    early, late = 49152 * EARLY, 49152 * (PART - EARLY)
     put(("X", 0), ["B"], 0.3, [
-        ("outer", "z0", 1, 49152), ("p0", "x0", 1, early), ("p1", "x0", 1, early),
-        ("m0", "x1", 1, early), ("m1", "x1", 1, early),
+        ("w0", "z0", 1, 49152), ("w1", "z0", 1, 49152), ("p0", "x0", 1, 98304), ("p1", "x0", 1, 98304),
+        ("m0", "x1", 1, 98304), ("m1", "x1", 1, 98304),
     ])
-    put(("X", 1), ["outer"], 0.2, [
-        ("po", "x0", 1, 98304), ("mo", "x1", 1, 98304), ("p2", "x0", 1, late), ("p3", "x0", 1, late),
-        ("m2", "x1", 1, late), ("m3", "x1", 1, late),
-    ])
-    put(("X", 2), ["p0"], 0.1, [("f0", "x0", 1, early)])
-    put(("X", 3), ["m1"], 0.1, [("f1", "x1", 1, early)])
-    put(("X", 4), ["po", "mo", ("X", 2), ("X", 3)], 0.1, [("f2", "x0", 1, 49152), ("f3", "x1", 1, 49152)])
-    put(("X", 6), ["f0"], 0.2, None)
-    put(("X", 5), ["p2", "m3", ("X", 4)], 0.1, [("f4", "x0", 1, late), ("f5", "x1", 1, late)])
-    feeds = {0: [("X", 1)], 1: ["m0", "m1", "mo"], 3: ["p0", "p1", "po"], 2: ["f0", "f1", "f2", "f3"]}
-    rest = {0: [], 1: ["m2", "m3"], 3: ["p2", "p3"], 2: ["f4", "f5"]}
+    put(("X", 1), ["w0"], 0.5, [("c0", "c", -1.5, 16000)])
+    put(("X", 5), ["w1"], 0.5, [("c1", "c", -1.5, 16000)])
+    put(("X", 2), ["p0"], 0.1, [("f0", "x0", 1, 98304)])
+    put(("X", 3), ["m1"], 0.1, [("f1", "x1", 1, 98304)])
+    put(("X", 4), ["f0"], 0.2, None)
+    feeds = {0: [], 1: ["m0", "m1"], 3: ["p0", "p1"], 2: ["f0", "f1"]}
     for u, (r, h, first, direct) in enumerate(units):
         h1, h2 = RING[first] // 2, RING[OTHER[first]] // 2
         size = BLOCK[first] * FEAT * 2
-        put(("M", u), feeds[r] + (rest[r] if h >= EARLY else []), 0.45)
+        put(("M", u, 0), feeds[r] + ["c0"], 0.25)
+        put(("M", u, 1), [("M", u, 0), "c1"], 0.2)
         for k in range(h1):
             for s in (0, 1):
-                needs = [("M", u)] + ([("R1", u, s, k - 1)] if k else [])
+                needs = [("M", u, s)] if k == 0 else [("M", u, 0), ("M", u, 1), ("R1", u, s, k - 1)]
                 sent = size // 2 if k == 0 else size
                 put(("S1", u, s, k), needs, 0.1, [(("R1", u, s, k), first + str(s), 1, sent)])
-        put(("F1", u), [("R1", u, 0, h1 - 1), ("R1", u, 1, h1 - 1)], 0.15)
+        put(("F1", u), [("M", u, 1), ("R1", u, 0, h1 - 1), ("R1", u, 1, h1 - 1)], 0.15)
         routes, ends = second_routes(u, units)
         for key, s, hops, _, adds in routes:
             needs = [("F1", u)] + ([("R2", u, adds)] if adds is not None else [])
@@ -128,7 +122,7 @@
                     best = ((key, rank(name)), name, at)
         _, name, at = best
         _, spent, out = tasks.pop(name)
-        now = max(now, at) + spent
+        now = max(now, at) + 0.5 * spent
         done[name] = now
         order.append(name)
         for label, link, hops, size in out or []:
@@ -140,7 +134,7 @@
     return order
 
 
-def attend(len_ref, own_ref, proj_ref, group, core, att):
+def attend(len_ref, own_ref, proj_ref, group, att):
     lens = [len_ref[j] for j in range(IMGS)]
     ends = [lens[0], lens[0] + lens[1], lens[0] + lens[1] + lens[2]]
     starts = [jnp.int32(0)] + ends
@@ -169,25 +163,31 @@
         totals = jnp.sum(raised, axis=-1, keepdims=True)
         weights = (raised / totals).astype(BF16)
         out = jnp.dot(weights, proj_ref[2, :, lanes], preferred_element_type=F32)
-        att[:, lanes] = out.astype(BF16)
-
-    stays = jnp.zeros((ROWS, ROWS), jnp.bool_)
+        att[h // PART, h % PART] = out.astype(BF16)
+
+    row256 = lax.broadcasted_iota(jnp.int32, (ROWS, PACK), 0)
+    col256 = lax.broadcasted_iota(jnp.int32, (ROWS, PACK), 1)
+    stays = jnp.zeros((ROWS, PACK), jnp.bool_)
     for j in range(IMGS):
-        stays = stays | ((row >= starts[j]) & (row < stops[j]) & (own_ref[j] == group))
-    picks = [jnp.where((row == col) & stays, 1.0, 0.0).astype(BF16)]
+        stays = stays | ((row256 >= starts[j]) & (row256 < stops[j]) & (own_ref[j] == group))
+    lands = (row256 == col256) & stays
+    picks = [jnp.where((row == col) & stays[:, :ROWS], 1.0, 0.0).astype(BF16)]
     row64 = lax.broadcasted_iota(jnp.int32, (SPAN, ROWS), 0)
     col64 = lax.broadcasted_iota(jnp.int32, (SPAN, ROWS), 1)
-    for target in (group + 1 - 2 * core, group + GROUPS - 1 + 2 * core):
+    for n, step in enumerate((1, GROUPS - 1)):
+        target = (group + step) % GROUPS
         first = jnp.int32(0)
         stop = jnp.int32(0)
         for j in range(IMGS):
-            chosen = own_ref[j] == target % GROUPS
+            chosen = own_ref[j] == target
             first = first + jnp.where(chosen, starts[j], 0)
             stop = stop + jnp.where(chosen, stops[j], 0)
         corner = jnp.minimum(first, ROWS - SPAN)
         pick = (col64 == row64 + corner) & (col64 >= first) & (col64 < stop)
         picks.append(jnp.where(pick, 1.0, 0.0).astype(BF16))
-    return picks
+        moves = (row256 >= first) & (row256 < stop)
+        lands = lands | ((col256 == row256 - corner + ROWS + SPAN * n) & moves)
+    return picks, jnp.where(lands, 1.0, 0.0).astype(BF16)
 
 
 def order_matrix(y, z, first):
@@ -206,21 +206,27 @@
 
 def kernel(
     steps, len_ref, own_ref, proj_hbm, cot_ref, att_out, grad_out,
-    proj_ref, att, att_all, outb, extra, cotb, gathered, order, partial, sum1_out, sum1_in, sum2, sum2_out, sum2_in, final, result,
+    proj_ref, att, att_all, leave, cot_own, cotb, gathered, order, turned, partial, sum1_out, sum1_in, sum2, sum2_out, sum2_in, final, result,
     send_sem, recv_sem, local_sem,
 ):
     y, z, core, x = place()
     other = 1 - core
     chip = y * NZ + z
     group = chip * 2 + core
-    after = (chip + 1) % (NY * NZ)
-    before = (chip + NY * NZ - 1) % (NY * NZ)
+    right = ((group + 1) % GROUPS, x)
+    left = ((group + GROUPS - 1) % GROUPS, x)
     sibling = device(y, z, other, x)
 
+    def half_of(c, which):
+        return (c // NZ + c % NZ + which) % 2
+
+    part = half_of(chip, core)
+    rest = 1 - part
+
     def shifted(axis, by, which=None):
-        c = core if which is None else which
         if axis == "x":
-            return device(y, z, c, x + by % NX)
+            return device(y, z, core if which is None else which, x + by % NX)
+        c = (core + by) % 2
         if axis == "y":
             return device(y + by % NY, z, c, x)
         return device(y, z + by % NZ, c, x)
@@ -229,7 +235,7 @@
     partners += [shifted("y", by) for by in range(1, NY)]
     partners += [shifted("z", by) for by in range(1, NZ)]
     partners += [shifted("x", by, which) for by in range(1, NX) for which in (0, 1)]
-    partners += [(c * 2 + which, x) for c in (after, before) for which in (0, 1)]
+    partners += [left, right]
     barrier = pltpu.get_barrier_semaphore()
     for p in partners:
         pl.semaphore_signal(barrier, inc=1, device_id=p, device_id_type=MESH)
@@ -271,41 +277,19 @@
     def rows(start, size):
         return pl.ds(pl.multiple_of(start, 64), size)
 
-    mine = ROWS + SPAN
-    own_rows = rows(core * mine, mine)
-    outer_at = 2 * mine
-    cot_pieces = [
-        (pl.ds(0, ROWS), rows(core * mine, ROWS)),
-        (pl.ds(ROWS, SPAN), rows(other * outer_at + core * ROWS, SPAN)),
-        (pl.ds(ROWS + SPAN, SPAN), rows(other * (mine + ROWS) + core * (outer_at + SPAN), SPAN)),
-    ]
-    cot_here = []
-    for n, (src, dst) in enumerate(cot_pieces):
-        copy = pltpu.make_async_copy(cot_ref.at[src], cotb.at[dst], local_sem.at[n])
-        copy.start()
-        cot_here.append(copy)
+    own_rows = rows(core * ROWS, ROWS)
+    cot_here = pltpu.make_async_copy(cot_ref.at[pl.ds(0, ROWS)], cot_own.at[pl.ds(0, ROWS)], local_sem.at[0])
+    cot_here.start()
 
     for copy in loads:
         copy.wait()
-    picks = attend(len_ref, own_ref, proj_ref, group, core, att)
-    start = 0
-    for pick in picks:
-        part = jnp.dot(pick, att[...], preferred_element_type=F32).astype(BF16)
-        for h in range(HEADS):
-            outb[h // PART, h % PART, start : start + pick.shape[0]] = part[:, h * HD : (h + 1) * HD]
-        start += pick.shape[0]
+    picks, lands = attend(len_ref, own_ref, proj_ref, group, att)
     for h in range(PART):
-        gathered[0, h, own_rows] = outb[core, h, 0:mine]
+        gathered[0, h, own_rows] = att[part, h]
     for n, first in enumerate(("y", "z")):
         order[n] = order_matrix(y, z, first)
 
     pl.semaphore_wait(barrier, len(partners))
-
-    outer_chip = before * other + after * core
-    outer_rows = [pl.ds(outer_at, SPAN), pl.ds(outer_at + SPAN, SPAN)]
-    every = pl.ds(0, PART)
-    first_heads = pl.ds(0, EARLY)
-    last_heads = pl.ds(EARLY, PART - EARLY)
 
     def crossing(sends, lands):
         base = fresh()
@@ -314,30 +298,37 @@
             message(*sends(which), base + core)
         return [landing(lands(which), base + which) for which in (0, 1)]
 
-    outer_dst = rows(outer_at + SPAN * other, SPAN)
-    outer = crossing(
-        lambda which: (
-            outb.at[which, every, pl.ds(mine, SPAN)], gathered.at[0, every, outer_dst], (outer_chip * 2 + which, x)
-        ),
-        lambda which: gathered.at[0, every, outer_rows[1 - which]],
-    )
-    inner_cp = message(outb.at[other, every, pl.ds(0, mine)], gathered.at[0, every, own_rows], sibling)
-    cot_there = [message(cot_ref.at[src], cotb.at[dst], sibling) for src, dst in cot_pieces]
-
-    def send_across(heads):
-        return {
-            slot: crossing(
-                lambda which: (
-                    outb.at[which, heads, pl.ds(0, mine)], gathered.at[slot, heads, own_rows],
-                    shifted("x", by, which),
-                ),
-                lambda which: gathered.at[slot, heads, pl.ds(which * mine, mine)],
-            )
-            for slot, by in ((3, 1), (1, 3))
-        }
-
-    across = {0: send_across(first_heads)}
-    extra_inner = message(outb.at[core, every, pl.ds(ROWS, SPAN)], extra.at[0], sibling)
+    halves = [pl.ds(0, FEAT // 2), pl.ds(FEAT // 2, FEAT // 2)]
+    windows = []
+    for half in halves:
+        first = (pl.ds(ROWS, SPAN), half)
+        second = (pl.ds(ROWS + SPAN, SPAN), half)
+        windows.append([
+            message(cot_ref.at[first], cot_own.at[first], left),
+            message(cot_ref.at[second], cot_own.at[second], right),
+        ])
+    across = {
+        slot: crossing(
+            lambda which: (
+                att.at[half_of(chip, which)], gathered.at[slot, :, own_rows], shifted("x", by, which)
+            ),
+            lambda which: gathered.at[slot, :, pl.ds(which * ROWS, ROWS)],
+        )
+        for slot, by in ((3, 1), (1, 3))
+    }
+    beside = message(att.at[rest], gathered.at[0, :, own_rows], sibling)
+
+    for n, pick in enumerate(picks):
+        for h in range(HEADS):
+            chosen = jnp.dot(pick, att[h // PART, h % PART], preferred_element_type=F32).astype(BF16)
+            if n == 0:
+                att_all[0:ROWS, h * HD : (h + 1) * HD] = chosen
+            else:
+                leave[n - 1, :, h * HD : (h + 1) * HD] = chosen
+    came = [
+        message(leave.at[0], att_all.at[pl.ds(ROWS, SPAN)], right),
+        message(leave.at[1], att_all.at[pl.ds(ROWS + SPAN, SPAN)], left),
+    ]
 
     waited = set()
     leaving = []
@@ -353,71 +344,47 @@
         by = 1 if slot == 3 else 3
         moved[label] = message(gathered.at[slot, heads, part], gathered.at[2, heads, part], shifted("x", by))
 
-    def write_attended():
-        arrived(extra_inner)
-        arrived(moved["extra"])
-        from_inner = rows(ROWS + SPAN * other, SPAN)
-        from_outer = rows(ROWS + SPAN * core, SPAN)
-        for h in range(HEADS):
-            att_all[0:ROWS, h * HD : (h + 1) * HD] = outb[h // PART, h % PART, 0:ROWS]
-        for h in range(PART):
-            here = pl.ds(pl.multiple_of(core * HALF + h * HD, HD), HD)
-            there = pl.ds(pl.multiple_of(other * HALF + h * HD, HD), HD)
-            att_all[from_inner, here] = gathered[0, h, rows(other * mine + ROWS, SPAN)]
-            att_all[from_inner, there] = extra[0, h]
-            att_all[from_outer, here] = gathered[0, h, rows(outer_at + SPAN * core, SPAN)]
-            att_all[from_outer, there] = extra[1, h]
-        copy = pltpu.make_async_copy(att_all, att_out, local_sem.at[6])
-        copy.start()
-        leaving.append(copy)
-
     def do_move(n):
-        if n == 6:
-            write_attended()
-        elif n == 1:
-            for copy in outer:
-                arrived(copy)
-            both = pl.ds(outer_at, 2 * SPAN)
-            moved["po"] = message(gathered.at[0, every, both], gathered.at[3, every, both], shifted("x", 1))
-            moved["mo"] = message(gathered.at[0, every, both], gathered.at[1, every, both], shifted("x", 3))
-            across[1] = send_across(last_heads)
-            arrived(inner_cp)
-            theirs = rows(outer_at + SPAN * other, SPAN)
-            moved["extra"] = message(gathered.at[0, every, theirs], extra.at[1], sibling)
+        if n in (1, 5):
+            which = 0 if n == 1 else 1
+            if which == 0:
+                cot_here.wait()
+            for copy in windows[which]:
+                copy.wait_recv()
+            spot = (own_rows, halves[which])
+            cotb[spot] = jnp.dot(lands, cot_own[:, halves[which]], preferred_element_type=F32).astype(BF16)
+            moved["c", which] = message(cotb.at[spot], cotb.at[spot], sibling)
         elif n == 2:
-            arrived(across[0][3][0])
-            forward("f0", 3, first_heads, pl.ds(0, mine))
+            arrived(across[3][0])
+            part_rows = pl.ds(0, ROWS)
+            moved["f0"] = message(gathered.at[3, :, part_rows], gathered.at[2, :, part_rows], shifted("x", 1))
         elif n == 3:
-            arrived(across[0][1][1])
-            forward("f1", 1, first_heads, pl.ds(mine, mine))
+            arrived(across[1][1])
+            part_rows = pl.ds(ROWS, ROWS)
+            moved["f1"] = message(gathered.at[1, :, part_rows], gathered.at[2, :, part_rows], shifted("x", 3))
         elif n == 4:
-            arrived(moved["po"])
-            arrived(moved["mo"])
-            forward("f2", 3, every, outer_rows[0])
-            forward("f3", 1, every, outer_rows[1])
-        elif n == 5:
-            arrived(across[1][3][0])
-            arrived(across[1][1][1])
-            forward("f4", 3, last_heads, pl.ds(0, mine))
-            forward("f5", 1, last_heads, pl.ds(mine, mine))
-
-    def do_multiply(u):
+            for copy in came:
+                copy.wait_recv()
+            copy = pltpu.make_async_copy(att_all, att_out, local_sem.at[6])
+            copy.start()
+            leaving.append(copy)
+
+    def do_multiply(u, half):
         r, h, first, _ = UNITS[u]
-        if r == 2:
-            for label in ("f0", "f1", "f2", "f3") + (("f4", "f5") if h >= EARLY else ()):
-                arrived(moved[label])
-        elif r:
-            for copy in across[0][r] + (across[1][r] if h >= EARLY else []):
-                arrived(copy)
-            arrived(moved["po" if r == 3 else "mo"])
-        turned = lax.dot_general(
-            order["yz".index(first)], gathered[r, h], (((1,), (1,)), ((), ())), preferred_element_type=F32
-        ).astype(BF16)
-        while cot_here:
-            cot_here.pop().wait()
-        for copy in cot_there:
-            arrived(copy)
-        partial[u] = jnp.dot(turned, cotb[...], preferred_element_type=F32)
+        if half == 0:
+            if r == 2:
+                arrived(moved["f0"])
+                arrived(moved["f1"])
+            elif r:
+                for copy in across[r]:
+                    arrived(copy)
+            else:
+                arrived(beside)
+            turned[u] = lax.dot_general(
+                order["yz".index(first)], gathered[r, h], (((1,), (1,)), ((), ())), preferred_element_type=F32
+            ).astype(BF16)
+        arrived(moved["c", half])
+        partial[u, :, halves[half]] = jnp.dot(turned[u], cotb[:, halves[half]], preferred_element_type=F32)
 
     received = {}
     shared = {}
@@ -502,14 +469,14 @@
         final[u, 1] = total[STACK // 2 :]
         here = result_rows(u, x)
         if r == 0:
-            result[core, here] = final[u, core]
-            copy = message(final.at[u, other], result.at[core, here], sibling)
+            result[part, here] = final[u, core]
+            copy = message(final.at[u, other], result.at[part, here], sibling)
             arriving.append((copy, here))
             return
         n = fresh()
         there = result_rows(u, (x + NX - r) % NX)
         for which in (0, 1):
-            message(final.at[u, which], result.at[core, here], shifted("x", r, which), n)
+            message(final.at[u, which], result.at[part, here], shifted("x", r, which), n)
         arriving.append((landing(result.at[:, there], n), there))
 
     run = {"X": do_move, "M": do_multiply, "S1": do_first, "F1": do_turn, "S2": do_second, "F2": do_last}
@@ -528,7 +495,7 @@
 
 
 def receive_count(units):
-    count = 24
+    count = 15
     for u, (_, _, first, direct) in enumerate(units):
         count += RING[first] - 1 + (1 if direct else len(second_routes(u, units)[0])) + 1
     return count
@@ -548,13 +515,14 @@
     anywhere = pl.BlockSpec(memory_space=pl.ANY)
     scratch = [
         pltpu.VMEM((3, ROWS, WIDTH), BF16),
-        pltpu.VMEM((ROWS, WIDTH), BF16),
+        pltpu.VMEM((2, PART, ROWS, HD), BF16),
         pltpu.VMEM((PACK, WIDTH), BF16),
-        pltpu.VMEM((2, PART, PACK, HD), BF16),
-        pltpu.VMEM((2, PART, SPAN, HD), BF16),
-        pltpu.VMEM((2 * PACK, FEAT), BF16),
-        pltpu.VMEM((NX, PART, 2 * PACK, HD), BF16),
+        pltpu.VMEM((2, SPAN, WIDTH), BF16),
+        pltpu.VMEM((PACK, FEAT), BF16),
+        pltpu.VMEM((2 * ROWS, FEAT), BF16),
+        pltpu.VMEM((NX, PART, 2 * ROWS, HD), BF16),
         pltpu.VMEM((2, HD, HD), BF16),
+        pltpu.VMEM((units, HD, 2 * ROWS), BF16),
         pltpu.VMEM((units, HD, FEAT), F32),
         pltpu.VMEM((units, 2, HD // 2, FEAT), BF16),
         pltpu.VMEM((units, 2, HD // 2, FEAT), BF16),

time: 60.7 us -> 60 us (0.988)
  Pallas kernels: 59.9 us -> 59.2 us
    pallas_call x1, Pallas kernels: 57.9 us -> 57.3 us  [shards(): pl.pallas_call(functools.partial(kernel, steps), out_shape=(jax.ShapeDtyp...]
where the time goes in v4:
time: 60 us; the launch traced here: 59.8 us
  Pallas kernels  59.2 us (99%)
  between operations  0.64 us (1%)
    pallas_call x1, Pallas kernels, shards(): pl.pallas_call(functools.partial(kernel, steps), out_shape=(jax.ShapeDtyp...  57.3 us
    pallas_call x1, Pallas kernels, shards(): pl.pallas_call(hand_over, out_shape=(jax.ShapeDtypeStruct(attended.shape,...  1.95 us

profile of v4, /device:TPU:1, one launch (start us, length us, event | category | flops | bytes accessed | tf_op | source)
XLA Modules:
  0.0 59.8 jit_solution(11703749563340416887)
XLA Ops:
  0.6 57.3 %attend_and_reduce.1 = (bf16[256,768]{1,0:T(8,128)(2,1)}, f32[2,288,128]{2,1,0:T(8,128)}) custom-call(s32[4]{0:T(128)} %len_ref.1, s32[4]{0:T(128)} %own_ref.1, bf16[3,128,768]{2,1,0:T(8,128)(2,1)} %proj_hbm.1, bf16[256,1536]{1,0:T(8,128)(2,1)} %cot_ref.1), custom_call_target="tpu_custom_call" | custom-call | tf_op jit(solution)/shard_map/attend_and_reduce/pallas_call | solution.py:538
  57.9 2.0 %hand_over.1 = (bf16[256,768]{1,0:T(8,128)(2,1)}, f32[2,288,128]{2,1,0:T(8,128)}) custom-call(bf16[256,768]{1,0:T(8,128)(2,1)} %get-tuple-element.6.attended_in, f32[2,288,128]{2,1,0:T(8,128)} %get-tuple-element.7.grads_in), custom_call_target="tpu_custom_call" | custom-call | tf_op jit(solution)/shard_map/hand_over/pallas_call | solution.py:552

commit v5 on v4

--- a/solution.py
+++ b/solution.py
@@ -205,8 +205,8 @@
 
 
 def kernel(
-    steps, len_ref, own_ref, proj_hbm, cot_ref, att_out, grad_out,
-    proj_ref, att, att_all, leave, cot_own, cotb, gathered, order, turned, partial, sum1_out, sum1_in, sum2, sum2_out, sum2_in, final, result,
+    steps, len_hbm, own_hbm, proj_hbm, cot_ref, att_out, grad_out,
+    len_ref, own_ref, proj_ref, att, att_all, leave, cot_own, cotb, gathered, order, turned, partial, sum1_out, sum1_in, sum2, sum2_out, sum2_in, final, result,
     send_sem, recv_sem, local_sem,
 ):
     y, z, core, x = place()
@@ -240,7 +240,12 @@
     for p in partners:
         pl.semaphore_signal(barrier, inc=1, device_id=p, device_id_type=MESH)
 
-    loads = []
+    loads = [
+        pltpu.make_async_copy(len_hbm, len_ref, local_sem.at[1]),
+        pltpu.make_async_copy(own_hbm, own_ref, local_sem.at[2]),
+    ]
+    for copy in loads:
+        copy.start()
     for n in range(3):
         copy = pltpu.make_async_copy(proj_hbm.at[n], proj_ref.at[n], local_sem.at[3 + n])
         copy.start()
@@ -511,9 +516,10 @@
     units = len(UNITS)
     messages = receive_count(UNITS)
     vmem = pl.BlockSpec(memory_space=pltpu.VMEM)
-    smem = pl.BlockSpec(memory_space=pltpu.SMEM)
     anywhere = pl.BlockSpec(memory_space=pl.ANY)
     scratch = [
+        pltpu.SMEM((IMGS,), jnp.int32),
+        pltpu.SMEM((IMGS,), jnp.int32),
         pltpu.VMEM((3, ROWS, WIDTH), BF16),
         pltpu.VMEM((2, PART, ROWS, HD), BF16),
         pltpu.VMEM((PACK, WIDTH), BF16),
@@ -541,7 +547,7 @@
             jax.ShapeDtypeStruct((PACK, WIDTH), BF16),
             jax.ShapeDtypeStruct((2, HEADS * D // HD, HD), F32),
         ),
-        in_specs=[smem, smem, anywhere, anywhere],
+        in_specs=[anywhere] * 4,
         out_specs=(anywhere, anywhere),
         scratch_shapes=scratch,
         compiler_params=pltpu.CompilerParams(

time: 60 us -> 59.3 us (0.988)
  Pallas kernels: 59.2 us -> 58.5 us
    pallas_call x1, Pallas kernels: 57.3 us -> 56.6 us  [shards(): pl.pallas_call(functools.partial(kernel, steps), out_shape=(jax.ShapeDtyp...]
where the time goes in v5:
time: 59.3 us; the launch traced here: 59.2 us
  Pallas kernels  58.5 us (99%)
  between operations  0.64 us (1%)
    pallas_call x1, Pallas kernels, shards(): pl.pallas_call(functools.partial(kernel, steps), out_shape=(jax.ShapeDtyp...  56.6 us
    pallas_call x1, Pallas kernels, shards(): pl.pallas_call(hand_over, out_shape=(jax.ShapeDtypeStruct(attended.shape,...  1.95 us

profile of v5, /device:TPU:1, one launch (start us, length us, event | category | flops | bytes accessed | tf_op | source)
XLA Modules:
  0.0 59.2 jit_solution(899405650133514049)
XLA Ops:
  0.6 56.6 %attend_and_reduce.1 = (bf16[256,768]{1,0:T(8,128)(2,1)}, f32[2,288,128]{2,1,0:T(8,128)}) custom-call(s32[4]{0:T(128)} %len_hbm.1, s32[4]{0:T(128)} %own_hbm.1, bf16[3,128,768]{2,1,0:T(8,128)(2,1)} %proj_hbm.1, bf16[256,1536]{1,0:T(8,128)(2,1)} %cot_ref.1), custom_call_target="tpu_custom_call" | custom-call | tf_op jit(solution)/shard_map/attend_and_reduce/pallas_call | solution.py:544
  57.2 2.0 %hand_over.1 = (bf16[256,768]{1,0:T(8,128)(2,1)}, f32[2,288,128]{2,1,0:T(8,128)}) custom-call(bf16[256,768]{1,0:T(8,128)(2,1)} %get-tuple-element.6.attended_in, f32[2,288,128]{2,1,0:T(8,128)} %get-tuple-element.7.grads_in), custom_call_target="tpu_custom_call" | custom-call | tf_op jit(solution)/shard_map/hand_over/pallas_call | solution.py:558
